TPU v7x, 32 devices: a whole 2x2x4 slice. The times are simulated.
32 devices in a mesh: rep: 2 (over y), fsdp: 16 (over z, x, core).
Axes of the slice: x: 2, y: 2, z: 4, core: 2. Of those that a mesh axis runs over, the one named last changes fastest.
Arguments:
- tokens: bfloat16 [37632, 768], P(('rep', 'fsdp')), may hold values from -6 to 6
- mask_flags: int32 [192, 196], P(('rep', 'fsdp')), may hold values 0 or 1
- mask_token: bfloat16 [768], P('fsdp'), may hold values from -4 to 4
- norm1_gain: bfloat16 [768], P('fsdp'), may hold values from 0.099609375 to 1.8984375
- norm1_bias: bfloat16 [768], P('fsdp'), may hold values from -1.5 to 1.5
- qkv_weight: bfloat16 [768, 2304], P('fsdp'), may hold values from -0.21875 to 0.21875
- query_bias: bfloat16 [768], P('fsdp'), may hold values from -1.5 to 1.5
- value_bias: bfloat16 [768], P('fsdp'), may hold values from -1.5 to 1.5
- proj_weight: bfloat16 [768, 768], P('fsdp'), may hold values from -1.75 to 1.75
- proj_bias: bfloat16 [768], P('fsdp'), may hold values from -1.5 to 1.5
- norm2_gain: bfloat16 [768], P('fsdp'), may hold values from 0.099609375 to 1.8984375
- norm2_bias: bfloat16 [768], P('fsdp'), may hold values from -1.5 to 1.5
- fc1_weight: bfloat16 [768, 3072], P('fsdp'), may hold values from -0.21875 to 0.21875
- fc1_bias: bfloat16 [3072], P('fsdp'), may hold values from -1.5 to 1.5
- fc2_weight: bfloat16 [3072, 768], P('fsdp'), may hold values from -0.109375 to 0.109375
- fc2_bias: bfloat16 [768], P('fsdp'), may hold values from -1.5 to 1.5
- out_grad: bfloat16 [37632, 768], P(('rep', 'fsdp')), may hold values from -6 to 6
Outputs:
- block_out: bfloat16 [37632, 768], P(('rep', 'fsdp'))
- input_grad: float32 [37632, 768], P(('rep', 'fsdp'))
- grad_mask_token: float32 [768], P('fsdp')
- grad_norm1_gain: float32 [768], P('fsdp')
- grad_norm1_bias: float32 [768], P('fsdp')
- grad_qkv_weight: float32 [768, 2304], P('fsdp')
- grad_query_bias: float32 [768], P('fsdp')
- grad_value_bias: float32 [768], P('fsdp')
- grad_proj_weight: float32 [768, 768], P('fsdp')
- grad_proj_bias: float32 [768], P('fsdp')
- grad_norm2_gain: float32 [768], P('fsdp')
- grad_norm2_bias: float32 [768], P('fsdp')
- grad_fc1_weight: float32 [768, 3072], P('fsdp')
- grad_fc1_bias: float32 [3072], P('fsdp')
- grad_fc2_weight: float32 [3072, 768], P('fsdp')
- grad_fc2_bias: float32 [768], P('fsdp')
Inputs may be any that keep to these rules, and one draw needn't show every extreme that they name: `mask_flags`: 1 marks a patch replaced by the mask token.
All inputs are finite; a program needn't handle non-finite values. No bound on the sum of `mask_flags` on one device may be relied on, other than what follows from the above.
Results may differ from a plain program's by a relative error of at most 0.012.
Values may be sent and summed in bfloat16 or wider, within the bound.
No kernel may reach another device: no remote copies, remote signals or barrier semaphores. Data moves between devices by JAX's collectives and lax.ppermute only.
A program may use at most 256 MiB of HBM per device.

v0:
```python
import math

import jax
import jax.numpy as jnp
from jax import lax
from jax.sharding import PartitionSpec as P

HEADS = 12


def layer_norm(values, gain, shift):
    mean_row = jnp.mean(values, axis=-1, keepdims=True)
    centred = values - mean_row
    spread = jnp.mean(centred * centred, axis=-1, keepdims=True)
    return centred * lax.rsqrt(spread + 1e-06) * gain + shift


def exact_gelu(values):
    return jax.nn.gelu(values, approximate=False)


def inner_rows(left, right):
    return lax.dot_general(
        left, right, (((0,), (0,)), ((), ())), preferred_element_type=jnp.float32
    )


def outer_cols(left, right):
    return lax.dot_general(
        left, right, (((1,), (1,)), ((), ())), preferred_element_type=jnp.float32
    )


def local(
    tokens,
    mask_flags,
    mask_token,
    norm1_gain,
    norm1_bias,
    qkv_weight,
    query_bias,
    value_bias,
    proj_weight,
    proj_bias,
    norm2_gain,
    norm2_bias,
    fc1_weight,
    fc1_bias,
    fc2_weight,
    fc2_bias,
    out_grad,
):
    gathered = (
        lax.all_gather(qkv_weight, "fsdp", axis=0, tiled=True),
        lax.all_gather(proj_weight, "fsdp", axis=0, tiled=True),
        lax.all_gather(fc1_weight, "fsdp", axis=0, tiled=True),
        lax.all_gather(fc2_weight, "fsdp", axis=0, tiled=True),
        lax.all_gather(mask_token, "fsdp", axis=0, tiled=True),
        lax.all_gather(norm1_gain, "fsdp", axis=0, tiled=True),
        lax.all_gather(norm1_bias, "fsdp", axis=0, tiled=True),
        lax.all_gather(query_bias, "fsdp", axis=0, tiled=True),
        lax.all_gather(value_bias, "fsdp", axis=0, tiled=True),
        lax.all_gather(proj_bias, "fsdp", axis=0, tiled=True),
        lax.all_gather(norm2_gain, "fsdp", axis=0, tiled=True),
        lax.all_gather(norm2_bias, "fsdp", axis=0, tiled=True),
        lax.all_gather(fc1_bias, "fsdp", axis=0, tiled=True),
        lax.all_gather(fc2_bias, "fsdp", axis=0, tiled=True),
    )
    w_qkv, w_proj, w_up, w_down = (gathered[0], gathered[1], gathered[2], gathered[3])
    (
        token_row,
        gain_one,
        shift_one,
        bias_query,
        bias_value,
        bias_proj,
        gain_two,
        shift_two,
        bias_up,
        bias_down,
    ) = [member.astype(jnp.float32) for member in gathered[4:]]
    images, patches = mask_flags.shape
    row_count, model_width = tokens.shape
    head_dim = model_width // HEADS
    score_scale = 1.0 / math.sqrt(head_dim)
    chosen = mask_flags.reshape(row_count, 1) == 1
    block_in = jnp.where(chosen, token_row[None, :], tokens.astype(jnp.float32))
    norm_full, norm_one_back = jax.vjp(layer_norm, block_in, gain_one, shift_one)
    norm_one = norm_full.astype(jnp.bfloat16)
    qkv_bias = jnp.concatenate([bias_query, jnp.zeros_like(bias_query), bias_value])
    qkv_rows = (jnp.dot(norm_one, w_qkv, preferred_element_type=jnp.float32) + qkv_bias).astype(
        jnp.bfloat16
    )
    shaped = qkv_rows.reshape(images, patches, 3, HEADS, head_dim)
    queries = shaped[:, :, 0]
    key_rows = shaped[:, :, 1]
    value_rows = shaped[:, :, 2]
    scores = (
        jnp.einsum("bqhd,bkhd->bhqk", queries, key_rows, preferred_element_type=jnp.float32)
        * score_scale
    )
    peak_score = jnp.max(scores, axis=-1, keepdims=True)
    raised = jnp.exp(scores - peak_score)
    row_total = jnp.sum(raised, axis=-1, keepdims=True)
    log_total = peak_score + jnp.log(row_total)
    probs_low = (raised / row_total).astype(jnp.bfloat16)
    attended = jnp.einsum(
        "bhqk,bkhd->bqhd", probs_low, value_rows, preferred_element_type=jnp.float32
    )
    attended = attended.reshape(row_count, model_width).astype(jnp.bfloat16)
    residual = block_in + jnp.dot(attended, w_proj, preferred_element_type=jnp.float32) + bias_proj
    norm_full_two, norm_two_back = jax.vjp(layer_norm, residual, gain_two, shift_two)
    norm_two = norm_full_two.astype(jnp.bfloat16)
    hidden_pre = jnp.dot(norm_two, w_up, preferred_element_type=jnp.float32) + bias_up
    hidden_full, gelu_back = jax.vjp(exact_gelu, hidden_pre)
    hidden_act = hidden_full.astype(jnp.bfloat16)
    block_out = (
        residual + jnp.dot(hidden_act, w_down, preferred_element_type=jnp.float32) + bias_down
    ).astype(jnp.bfloat16)
    held = lax.optimization_barrier((qkv_weight, proj_weight, fc1_weight, fc2_weight, block_out))
    w_qkv, w_proj, w_up, w_down = (
        lax.all_gather(held[0], "fsdp", axis=0, tiled=True),
        lax.all_gather(held[1], "fsdp", axis=0, tiled=True),
        lax.all_gather(held[2], "fsdp", axis=0, tiled=True),
        lax.all_gather(held[3], "fsdp", axis=0, tiled=True),
    )
    grad_down = inner_rows(hidden_act, out_grad)
    grad_bias_down = jnp.sum(out_grad.astype(jnp.float32), axis=0)
    grad_act = outer_cols(out_grad, w_down)
    grad_pre = gelu_back(grad_act)[0].astype(jnp.bfloat16)
    grad_up = inner_rows(norm_two, grad_pre)
    grad_bias_up = jnp.sum(grad_pre.astype(jnp.float32), axis=0)
    grad_norm_two = outer_cols(grad_pre, w_up)
    back_resid, grad_gain_two, grad_shift_two = norm_two_back(grad_norm_two)
    grad_residual = out_grad.astype(jnp.float32) + back_resid
    resid_low = grad_residual.astype(jnp.bfloat16)
    grad_proj = inner_rows(attended, resid_low)
    grad_bias_proj = jnp.sum(grad_residual, axis=0)
    grad_attended = (
        outer_cols(resid_low, w_proj).astype(jnp.bfloat16).reshape(images, patches, HEADS, head_dim)
    )
    scores_again = (
        jnp.einsum("bqhd,bkhd->bhqk", queries, key_rows, preferred_element_type=jnp.float32)
        * score_scale
    )
    probs_again = jnp.exp(scores_again - log_total)
    probs_again_low = probs_again.astype(jnp.bfloat16)
    grad_values = jnp.einsum(
        "bhqk,bqhd->bkhd", probs_again_low, grad_attended, preferred_element_type=jnp.float32
    )
    grad_probs = jnp.einsum(
        "bqhd,bkhd->bhqk", grad_attended, value_rows, preferred_element_type=jnp.float32
    )
    row_inner = jnp.sum(probs_again * grad_probs, axis=-1, keepdims=True)
    grad_scores = (probs_again * (grad_probs - row_inner)).astype(jnp.bfloat16)
    grad_queries = (
        jnp.einsum("bhqk,bkhd->bqhd", grad_scores, key_rows, preferred_element_type=jnp.float32)
        * score_scale
    )
    grad_keys = (
        jnp.einsum("bhqk,bqhd->bkhd", grad_scores, queries, preferred_element_type=jnp.float32)
        * score_scale
    )
    grad_qkv = jnp.stack([grad_queries, grad_keys, grad_values], axis=2)
    grad_qkv = grad_qkv.reshape(row_count, 3 * model_width).astype(jnp.bfloat16)
    grad_attn_in = inner_rows(norm_one, grad_qkv)
    column_sums = jnp.sum(grad_qkv.astype(jnp.float32), axis=0)
    grad_bias_query = column_sums[:model_width]
    grad_bias_value = column_sums[2 * model_width :]
    grad_norm_one = outer_cols(grad_qkv, w_qkv)
    back_base, grad_gain_one, grad_shift_one = norm_one_back(grad_norm_one)
    grad_base = grad_residual + back_base
    input_grad = jnp.where(chosen, 0.0, grad_base)
    grad_token = jnp.sum(jnp.where(chosen, grad_base, 0.0), axis=0)
    shares = (
        lax.psum_scatter(grad_token, "fsdp", scatter_dimension=0, tiled=True),
        lax.psum_scatter(grad_gain_one, "fsdp", scatter_dimension=0, tiled=True),
        lax.psum_scatter(grad_shift_one, "fsdp", scatter_dimension=0, tiled=True),
        lax.psum_scatter(grad_attn_in, "fsdp", scatter_dimension=0, tiled=True),
        lax.psum_scatter(grad_bias_query, "fsdp", scatter_dimension=0, tiled=True),
        lax.psum_scatter(grad_bias_value, "fsdp", scatter_dimension=0, tiled=True),
        lax.psum_scatter(grad_proj, "fsdp", scatter_dimension=0, tiled=True),
        lax.psum_scatter(grad_bias_proj, "fsdp", scatter_dimension=0, tiled=True),
        lax.psum_scatter(grad_gain_two, "fsdp", scatter_dimension=0, tiled=True),
        lax.psum_scatter(grad_shift_two, "fsdp", scatter_dimension=0, tiled=True),
        lax.psum_scatter(grad_up, "fsdp", scatter_dimension=0, tiled=True),
        lax.psum_scatter(grad_bias_up, "fsdp", scatter_dimension=0, tiled=True),
        lax.psum_scatter(grad_down, "fsdp", scatter_dimension=0, tiled=True),
        lax.psum_scatter(grad_bias_down, "fsdp", scatter_dimension=0, tiled=True),
    )
    totals = tuple(lax.psum(tuple(shares), "rep"))
    return (block_out, input_grad) + tuple(totals)


def solution(mesh):
    in_specs = (
        P(("rep", "fsdp"), None),
        P(("rep", "fsdp"), None),
        P("fsdp"),
        P("fsdp"),
        P("fsdp"),
        P("fsdp", None),
        P("fsdp"),
        P("fsdp"),
        P("fsdp", None),
        P("fsdp"),
        P("fsdp"),
        P("fsdp"),
        P("fsdp", None),
        P("fsdp"),
        P("fsdp", None),
        P("fsdp"),
        P(("rep", "fsdp"), None),
    )
    out_specs = (
        P(("rep", "fsdp"), None),
        P(("rep", "fsdp"), None),
        P("fsdp"),
        P("fsdp"),
        P("fsdp"),
        P("fsdp", None),
        P("fsdp"),
        P("fsdp"),
        P("fsdp", None),
        P("fsdp"),
        P("fsdp"),
        P("fsdp"),
        P("fsdp", None),
        P("fsdp"),
        P("fsdp", None),
        P("fsdp"),
    )
    return jax.shard_map(local, mesh=mesh, in_specs=in_specs, out_specs=out_specs, check_vma=False)
```

profile of v0, /device:TPU:0, one launch (start us, length us, event | category | flops | bytes accessed | tf_op | source)
XLA Modules:
  0.0 925.1 jit_solution(12305670244767503497)
XLA Ops:
  10.0 1.3 fusion.61
  13.5 0.8 dynamic-update-slice.6
  14.3 0.8 dynamic-update-slice.7
  15.2 0.8 dynamic-update-slice.5
  16.0 0.8 dynamic-update-slice
  16.8 0.8 dynamic-update-slice.1
  17.7 0.8 dynamic-update-slice.2
  18.5 0.8 dynamic-update-slice.3
  19.3 0.8 dynamic-update-slice.4
  20.2 0.8 dynamic-update-slice.9
  21.0 0.8 dynamic-update-slice.8
  21.9 63.5 %all-reduce.23 = (bf16[768]{0:T(1024)(128)(2,1)S(1)}, bf16[768]{0:T(1024)(128)(2,1)S(1)}, bf16[768]{0:T(1024)(128)(2,1)S(1)}, bf16[768]{0:T(1024)(128)(2,1)S(1)}...) all-reduce(bf16[768]{0:T(1024)(128)(2,1)S(1)} %dynamic-update-slice, ...), channel_id=1, replica_groups=mesh['rep'=2,'fsdp'=16] {'fsdp'}, use_global_device_ids=true, to_apply=%add.4 | all-reduce | flops 9984 | bytes 39936
  86.1 2.1 fusion.24
  88.2 2.4 multiply_reduce_fusion.7
  91.3 8.8 fusion.14
  100.2 17.1 %reshape.197 = bf16[6,196,3,12,64]{4,3,2,1,0:T(8,128)(2,1)} reshape(bf16[1176,2304]{1,0:T(8,128)(2,1)} %fusion.14) | data formatting | bytes 10838016 | tf_op jit(solution)/shard_map/reshape | solution.py:94
  117.3 11.4 %fusion.59 = (bf16[6,196,1,12,64]{4,3,2,1,0:T(8,128)(2,1)}, bf16[6,196,1,12,64]{4,3,2,1,0:T(8,128)(2,1)}, bf16[6,196,1,12,64]{4,3,2,1,0:T(8,128)(2,1)}) fusion(bf16[6,196,3,12,64]{4,3,2,1,0:T(8,128)(2,1)} %reshape.197), kind=kLoop, calls=%fused_computation.105 | loop fusion | bytes 10838016 | tf_op jit(solution)/shard_map/slice | solution.py:97
  128.7 6.8 copy.76
  135.4 6.8 copy.77
  142.3 6.1 copy.78
  148.4 9.9 %multiply_reduce_fusion.1 = (f32[6,12,196]{2,1,0:T(8,128)S(1)}, f32[6,12,196,196]{2,3,1,0:T(8,128)}) fusion(bf16[6,196,1,12,64]{1,4,3,0,2:T(8,128)(2,1)S(1)} %copy.78, bf16[6,196,1,12,64]{1,4,3,0,2:T(8,128)(2,1)} %copy.77), kind=kOutput, calls=%fused_computation.36 | convolution fusion | flops 359559648 | bytes 14732928 | tf_op jit(solution)/shard_map/bqhd,bkhd->bhqk/dot_general | solution.py:99
  158.3 9.1 fusion.13
  167.5 8.7 convert_bitcast_fusion
  176.2 3.4 copy.60
  179.5 6.0 convert_element_type.104
  185.6 3.9 fusion.62
  189.5 1.8 copy-done.8
  192.5 40.6 %multiply_convert_fusion.1 = (bf16[1176,3072]{1,0:T(8,128)(2,1)}, f32[1176,3072]{1,0:T(8,128)}, f32[1176,3072]{1,0:T(8,128)}) fusion(f32[3072]{0:T(1024)S(1)} %convert_element_type.109, bf16[768,3072]{1,0:T(8,128)(2,1)} %all-gather.13.cloned.1.call-done, f32[1176,768]{1,0:T(8,128)} %copy-done.8, f32[768]{0:T(1024)S(1)} %convert_element_type.107, ...), kind=kOutput, calls=%fused_computation.17 | convolution fusion | flops 5792016384 | bytes 44485824 | tf_op jit(solution)/shard_map/dot_general | solution.py:114
  233.1 11.0 %fusion.26 = bf16[1176,768]{1,0:T(8,128)(2,1)} fusion(f32[1176,768]{1,0:T(8,128)} %copy-done.8, bf16[1176,3072]{1,0:T(8,128)(2,1)} %get-tuple-element.72, bf16[3072,768]{1,0:T(8,128)(2,1)} %all-gather.15.cloned.1.call-done, f32[768]{0:T(1024)S(1)} %copy-done.36), kind=kOutput, calls=%fused_computation.67 | convolution fusion | flops 5551773696 | bytes 17366016 | tf_op jit(solution)/shard_map/dot_general | solution.py:118
  245.5 49.4 %all-gather.17.cloned.1.call-done = bf16[3072,768]{1,0:T(8,128)(2,1)} async-done(((bf16[192,768]{1,0:T(8,128)(2,1)}), bf16[3072,768]{1,0:T(8,128)(2,1)}) %all-gather.17.cloned.1.call-update) | async-done | bytes 4718608 | tf_op jit(solution)/shard_map/all_gather | solution.py:125
  294.9 19.2 %convert_reduce_fusion = (f32[3072]{0:T(1024)S(1)}, bf16[1176,3072]{1,0:T(8,128)(2,1)}) fusion(f32[1176,3072]{1,0:T(8,128)} %get-tuple-element.73, f32[1176,3072]{1,0:T(8,128)} %get-tuple-element.88, bf16[3072,768]{1,0:T(8,128)(2,1)} %all-gather.17.cloned.1.call-done, bf16[1176,768]{1,0:T(8,128)(2,1)S(1)} %copy-done.13), kind=kOutput, calls=%fused_computation.16 | convolution fusion | flops 5606863872 | bytes 42663936 | tf_op jit(solution)/shard_map/dot_general | solution.py:29
  314.1 34.7 %all-gather.19.cloned.1.call-done = bf16[768,3072]{1,0:T(8,128)(2,1)} async-done(((bf16[48,3072]{1,0:T(8,128)(2,1)}), bf16[768,3072]{1,0:T(8,128)(2,1)}) %all-gather.19.cloned.1.call-update) | async-done | bytes 4718608 | tf_op jit(solution)/shard_map/all_gather | solution.py:124
  348.9 12.4 %multiply_reduce_fusion.2 = (f32[768]{0:T(1024)S(1)}, f32[1176]{0:T(1024)S(1)}, f32[768]{0:T(1024)S(1)}, f32[1176,768]{1,0:T(8,128)S(1)}) fusion(f32[1176,768]{1,0:T(8,128)} %copy-done.8, f32[1176]{0:T(1024)S(1)} %fusion.50, f32[1176]{0:T(1024)S(1)} %broadcast_multiply_fusion, f32[768]{0:T(1024)S(1)} %convert_element_type.106, ...), kind=kOutput, calls=%fused_computation.53 | convolution fusion | flops 5556286464 | bytes 19192608 | tf_op jit(solution)/shard_map/dot_general | solution.py:29
  361.3 1.4 fusion.57
  363.3 1.8 copy-done.6
  365.1 3.2 fusion.46
  368.4 11.1 %fusion.63 = f32[3072,768]{1,0:T(8,128)} fusion(bf16[1176,3072]{1,0:T(8,128)(2,1)} %get-tuple-element.72, bf16[1176,768]{1,0:T(8,128)(2,1)S(1)} %copy-done.13), kind=kOutput, calls=%fused_computation.109 | convolution fusion | flops 5549064192 | bytes 18468864 | tf_op jit(solution)/shard_map/dot_general | solution.py:23
  380.4 7.7 all-gather.21.cloned.1.call-done
  388.1 4.0 convolution_convert_fusion
  392.1 4.2 reshape.198
  396.3 5.7 copy.62
  402.0 12.1 %multiply_reduce_fusion = (f32[6,12,196]{2,1,0:T(8,128)S(1)}, f32[6,12,196,196]{2,3,1,0:T(8,128)}) fusion(f32[6,12,196,196]{2,3,1,0:T(8,128)} %get-tuple-element.85, f32[6,12,196]{2,1,0:T(8,128)S(1)} %log_add_fusion, bf16[6,196,12,64]{1,3,2,0:T(8,128)(2,1)S(1)} %copy.62, bf16[6,196,1,12,64]{1,4,3,0,2:T(8,128)(2,1)} %copy.76), kind=kOutput, calls=%fused_computation.2 | convolution fusion | flops 365091552 | bytes 25853184 | tf_op jit(solution)/shard_map/bqhd,bkhd->bhqk/dot_general | solution.py:151
  414.1 11.1 %multiply_convert_fusion = bf16[6,12,196,196]{2,3,1,0:T(8,128)(2,1)S(1)} fusion(f32[6,12,196,196]{2,3,1,0:T(8,128)} %get-tuple-element.91, f32[6,12,196,196]{2,3,1,0:T(8,128)} %get-tuple-element.85, f32[6,12,196]{2,1,0:T(8,128)S(1)} %get-tuple-element.90, f32[6,12,196]{2,1,0:T(8,128)S(1)} %log_add_fusion), kind=kLoop, calls=%fused_computation.1 | loop fusion | flops 13829760 | bytes 27772416 | tf_op jit(solution)/shard_map/convert_element_type | solution.py:155
  425.2 3.8 multiply_bitcast_fusion
  429.1 2.9 multiply_bitcast_fusion.1
  432.0 8.2 fusion.37
  440.2 6.2 convert_reduce_fusion.1
  446.4 12.4 %copy.67 = bf16[6,196,3,12,64]{1,0,4,3,2:T(8,128)(2,1)} copy(bf16[6,196,3,12,64]{1,4,3,0,2:T(8,128)(2,1)} %get-tuple-element.67) | data formatting | bytes 10838016 | tf_op jit(solution)/shard_map/convert_element_type | solution.py:165
  458.8 15.1 %convert_element_type.120 = bf16[1176,2304]{0,1:T(8,128)(2,1)} reshape(bf16[6,196,3,12,64]{1,0,4,3,2:T(8,128)(2,1)} %copy.67) | data formatting | bytes 10838016 | tf_op jit(solution)/shard_map/convert_element_type | solution.py:165
  473.9 11.8 %fusion.54 = f32[768,2304]{1,0:T(8,128)} fusion(bf16[1176,2304]{0,1:T(8,128)(2,1)} %convert_element_type.120, bf16[1176,768]{1,0:T(8,128)(2,1)S(1)} %copy-done.5, f32[768]{0:T(1024)S(1)} %copy-done.35, f32[768]{0:T(1024)S(1)} %copy-done.31, f32[1176]{0:T(1024)S(1)} %copy-done.29, f32[1176]{0:T(1024)S(1)} %copy-done.23, f32[768]{0:T(1024)S(1)} %copy-done.25, ...), kind=kOutput, calls=%fused_computation.101 | convolution fusion | flops 4168120320 | bytes 14323032 | tf_op jit(solution)/shard_map/dot_general | solution.py:23
  486.4 12.9 %fusion.53 = f32[768,3072]{1,0:T(8,128)} fusion(bf16[1176,3072]{1,0:T(8,128)(2,1)} %get-tuple-element.94, f32[1176,768]{1,0:T(8,128)} %copy-done.8, f32[768]{0:T(1024)S(1)} %copy-done.33, f32[768]{0:T(1024)S(1)} %convert_element_type.106, f32[1176]{0:T(1024)S(1)} %fusion.50, f32[1176]{0:T(1024)S(1)} %broadcast_multiply_fusion), kind=kOutput, calls=%fused_computation.100 | convolution fusion | flops 5553580032 | bytes 20290752 | tf_op jit(solution)/shard_map/dot_general | solution.py:23
  501.3 67.5 %reduce-scatter.11.cloned.1.call-done = f32[192,768]{1,0:T(8,128)} async-done(((f32[3072,768]{1,0:T(8,128)}), f32[192,768]{1,0:T(8,128)}) %reduce-scatter.11.cloned.1.call-update) | async-done | bytes 589840 | tf_op jit(solution)/shard_map/reduce_scatter | solution.py:188
  568.9 93.6 %reduce-scatter.5.cloned.1.call-done = f32[48,2304]{1,0:T(8,128)} async-done(((f32[768,2304]{1,0:T(8,128)}), f32[48,2304]{1,0:T(8,128)}) %reduce-scatter.5.cloned.1.call-update) | async-done | bytes 442384 | tf_op jit(solution)/shard_map/reduce_scatter | solution.py:179
  662.5 115.6 %reduce-scatter.9.cloned.1.call-done = f32[48,3072]{1,0:T(8,128)} async-done(((f32[768,3072]{1,0:T(8,128)}), f32[48,3072]{1,0:T(8,128)}) %reduce-scatter.9.cloned.1.call-update) | async-done | bytes 589840 | tf_op jit(solution)/shard_map/reduce_scatter | solution.py:186
  778.1 49.1 %all-gather.23.cloned.1.call-done = bf16[768,2304]{1,0:T(8,128)(2,1)} async-done(((bf16[48,2304]{1,0:T(8,128)(2,1)}), bf16[768,2304]{1,0:T(8,128)(2,1)}) %all-gather.23.cloned.1.call-update) | async-done | bytes 3538960 | tf_op jit(solution)/shard_map/all_gather | solution.py:122
  827.2 11.6 %multiply_reduce_fusion.3 = (f32[768]{0:T(1024)S(1)}, f32[1176]{0:T(1024)S(1)}, f32[768]{0:T(1024)S(1)}, f32[1176,768]{1,0:T(8,128)}) fusion(bf16[1176,768]{1,0:T(8,128)(2,1)S(1)} %copy-done.5, f32[1176]{0:T(1024)S(1)} %copy-done.29, f32[1176]{0:T(1024)S(1)} %copy-done.23, f32[768]{0:T(1024)S(1)} %copy-done.25, pred[1176]{0:T(1024)(128)(4,1)S(1)} %copy-done.27, ...), kind=kOutput, calls=%fused_computation.54 | convolution fusion | flops 4170827008 | bytes 14404536 | tf_op jit(solution)/shard_map/dot_general | solution.py:29
  838.9 3.7 fusion.56
  842.6 2.4 fusion.55
  845.1 59.8 %all-reduce.20 = (f32[768]{0:T(1024)S(1)}, f32[768]{0:T(1024)S(1)}, f32[768]{0:T(1024)S(1)}, f32[768]{0:T(1024)S(1)}, f32[768]{0:T(1024)S(1)}, /*index=5*/f32[76...) all-reduce(f32[768]{0:T(1024)S(1)} %get-tuple-element.30, ...), channel_id=2, replica_groups=mesh['rep'=2,'fsdp'=16] {'fsdp'}, use_global_device_ids=true, to_apply=%region_12.13.clone | all-reduce | flops 9984 | bytes 79872
  905.6 5.6 all-reduce.21
  911.2 1.8 copy.93
  913.0 1.6 copy.94
  914.6 1.9 copy.95
  916.5 1.9 copy.96
  (152 shorter events, 11.4 us)
Async XLA Ops:
  7.2 84.1 %copy-start.3 = (bf16[1176,768]{1,0:T(8,128)(2,1)S(1)}, bf16[1176,768]{1,0:T(8,128)(2,1)}, u32[]{:S(2)}) copy-start(bf16[1176,768]{1,0:T(8,128)(2,1)} %param.17) | copy-start | bytes 5419012
  7.2 84.1 %all-gather.9.cloned.1.call-start = ((), (), s32[]{:S(2)}) async-start(), calls=%async_computation.4 | async-start | bytes 3760128 | tf_op jit(solution)/shard_map/all_gather | solution.py:54
  7.9 177.6 %all-gather.11.cloned.1.call-start = ((), (), s32[]{:S(2)}) async-start(), calls=%async_computation.5 | async-start | bytes 1253376 | tf_op jit(solution)/shard_map/all_gather | solution.py:55
  8.7 183.9 %all-gather.13.cloned.1.call-start = ((), (), s32[]{:S(2)}) async-start(), calls=%async_computation.6 | async-start | bytes 5013504 | tf_op jit(solution)/shard_map/all_gather | solution.py:56
  9.4 223.7 %all-gather.15.cloned.1.call-start = ((), (), s32[]{:S(2)}) async-start(), calls=%async_computation.7 | async-start | bytes 5013504 | tf_op jit(solution)/shard_map/all_gather | solution.py:57
  10.0 284.9 %all-gather.17.cloned.1.call-start = ((), (), s32[]{:S(2)}) async-start(), calls=%async_computation.8 | async-start | bytes 5013504 | tf_op jit(solution)/shard_map/all_gather | solution.py:125
  13.5 172.1 %copy-start.26 = (pred[1176]{0:T(1024)(128)(4,1)}, pred[1176]{0:T(1024)(128)(4,1)S(1)}, u32[]{:S(2)}) copy-start(pred[1176]{0:T(1024)(128)(4,1)S(1)} %eq.16) | copy-start | bytes 3532
  85.4 100.2 %copy-start.24 = (f32[768]{0:T(1024)}, f32[768]{0:T(1024)S(1)}, u32[]{:S(2)}) copy-start(f32[768]{0:T(1024)S(1)} %convert_element_type.93) | copy-start | bytes 9220
  85.4 14.7 %copy-start.30 = (f32[768]{0:T(1024)}, f32[768]{0:T(1024)S(1)}, u32[]{:S(2)}) copy-start(f32[768]{0:T(1024)S(1)} %convert_element_type.95) | copy-start | bytes 9220
  85.4 14.7 %copy-start.34 = (f32[768]{0:T(1024)}, f32[768]{0:T(1024)S(1)}, u32[]{:S(2)}) copy-start(f32[768]{0:T(1024)S(1)} %convert_element_type.96) | copy-start | bytes 9220
  85.4 107.1 %copy-start.32 = (f32[768]{0:T(1024)}, f32[768]{0:T(1024)S(1)}, u32[]{:S(2)}) copy-start(f32[768]{0:T(1024)S(1)} %convert_element_type.107) | copy-start | bytes 9220
  88.1 12.0 %copy-start.22 = (f32[1176]{0:T(1024)}, f32[1176]{0:T(1024)S(1)}, u32[]{:S(2)}) copy-start(f32[1176]{0:T(1024)S(1)} %broadcast_multiply_fusion.1) | copy-start | bytes 14116
  90.6 0.6 copy-start.18
  91.2 8.9 copy-start.28
  148.4 9.9 %copy-start = (bf16[6,196,1,12,64]{1,4,3,0,2:T(8,128)(2,1)}, bf16[6,196,1,12,64]{1,4,3,0,2:T(8,128)(2,1)S(1)}, u32[]{:S(2)}) copy-start(bf16[6,196,1,12,64]{1,4,3,0,2:T(8,128)(2,1)S(1)} %copy.78) | copy-start | bytes 5419012
  158.3 9.1 copy-start.14
  158.3 9.1 copy-start.10
  167.5 8.7 copy-start.16
  176.2 9.4 %copy-start.4 = (bf16[1176,768]{1,0:T(8,128)(2,1)S(1)}, bf16[1176,768]{1,0:T(8,128)(2,1)}, u32[]{:S(2)}) copy-start(bf16[1176,768]{1,0:T(8,128)(2,1)} %param.17) | copy-start | bytes 5419012
  189.5 1.8 copy-start.8
  191.9 0.6 copy-start.20
  192.5 40.6 %copy-start.36 = (f32[768]{0:T(1024)S(1)}, f32[768]{0:T(1024)}, u32[]{:S(2)}) copy-start(f32[768]{0:T(1024)} %convert_element_type.111) | copy-start | bytes 9220
  233.1 61.8 %copy-start.13 = (bf16[1176,768]{1,0:T(8,128)(2,1)S(1)}, bf16[1176,768]{1,0:T(8,128)(2,1)}, u32[]{:S(2)}) copy-start(bf16[1176,768]{1,0:T(8,128)(2,1)} %param.33) | copy-start | bytes 5419012
  244.2 104.7 %all-gather.19.cloned.1.call-start = ((), (), s32[]{:S(2)}) async-start(), calls=%async_computation.9 | async-start | bytes 5013504 | tf_op jit(solution)/shard_map/all_gather | solution.py:124
  244.7 143.3 %all-gather.21.cloned.1.call-start = ((), (), s32[]{:S(2)}) async-start(), calls=%async_computation.10 | async-start | bytes 1253376 | tf_op jit(solution)/shard_map/all_gather | solution.py:123
  245.5 255.8 %reduce-scatter.7.cloned.1.call-start = ((), (), s32[]{:S(2)}) async-start(), calls=%async_computation.13 | async-start | bytes 2506752 | tf_op jit(solution)/shard_map/reduce_scatter | solution.py:182
  348.9 12.4 %copy-start.21 = (f32[1176]{0:T(1024)S(1)}, f32[1176]{0:T(1024)}, u32[]{:S(2)}) copy-start(f32[1176]{0:T(1024)} %copy-done.20) | copy-start | bytes 14116
  348.9 12.4 %copy-start.9 = (f32[1176,768]{1,0:T(8,128)S(1)}, f32[1176,768]{1,0:T(8,128)}, u32[]{:S(2)}) copy-start(f32[1176,768]{1,0:T(8,128)} %copy-done.8) | copy-start | bytes 10838020
  362.7 2.5 copy-start.12
  363.3 1.8 copy-start.6
  368.3 200.5 %reduce-scatter.11.cloned.1.call-start = ((), (), s32[]{:S(2)}) async-start(), calls=%async_computation.15 | async-start | bytes 10027008 | tf_op jit(solution)/shard_map/reduce_scatter | solution.py:188
  379.4 0.9 copy-start.15
  379.4 0.9 copy-start.17
  379.5 283.0 %reduce-scatter.5.cloned.1.call-start = ((), (), s32[]{:S(2)}) async-start(), calls=%async_computation.12 | async-start | bytes 7520256 | tf_op jit(solution)/shard_map/reduce_scatter | solution.py:179
  414.1 11.1 %copy-start.2 = (bf16[6,196,1,12,64]{1,4,3,0,2:T(8,128)(2,1)S(1)}, bf16[6,196,1,12,64]{1,4,3,0,2:T(8,128)(2,1)}, u32[]{:S(2)}) copy-start(bf16[6,196,1,12,64]{1,4,3,0,2:T(8,128)(2,1)} %copy.77) | copy-start | bytes 5419012
  425.2 3.9 copy-start.1
  432.0 8.2 copy-start.11
  458.8 15.1 %copy-start.5 = (bf16[1176,768]{1,0:T(8,128)(2,1)S(1)}, bf16[1176,768]{1,0:T(8,128)(2,1)}, u32[]{:S(2)}) copy-start(bf16[1176,768]{1,0:T(8,128)(2,1)} %param.17) | copy-start | bytes 5419012
  458.8 15.1 %copy-start.23 = (f32[1176]{0:T(1024)S(1)}, f32[1176]{0:T(1024)}, u32[]{:S(2)}) copy-start(f32[1176]{0:T(1024)} %copy-done.22) | copy-start | bytes 14116
  458.8 15.1 %copy-start.25 = (f32[768]{0:T(1024)S(1)}, f32[768]{0:T(1024)}, u32[]{:S(2)}) copy-start(f32[768]{0:T(1024)} %copy-done.24) | copy-start | bytes 9220
  458.8 15.1 %copy-start.27 = (pred[1176]{0:T(1024)(128)(4,1)S(1)}, pred[1176]{0:T(1024)(128)(4,1)}, u32[]{:S(2)}) copy-start(pred[1176]{0:T(1024)(128)(4,1)} %copy-done.26) | copy-start | bytes 3532
  458.8 15.1 %copy-start.29 = (f32[1176]{0:T(1024)S(1)}, f32[1176]{0:T(1024)}, u32[]{:S(2)}) copy-start(f32[1176]{0:T(1024)} %copy-done.28) | copy-start | bytes 14116
  458.8 15.1 %copy-start.31 = (f32[768]{0:T(1024)S(1)}, f32[768]{0:T(1024)}, u32[]{:S(2)}) copy-start(f32[768]{0:T(1024)} %copy-done.30) | copy-start | bytes 9220
  458.8 15.1 %copy-start.35 = (f32[768]{0:T(1024)S(1)}, f32[768]{0:T(1024)}, u32[]{:S(2)}) copy-start(f32[768]{0:T(1024)} %copy-done.34) | copy-start | bytes 9220
  485.7 0.7 copy-start.33
  485.8 292.3 %reduce-scatter.9.cloned.1.call-start = ((), (), s32[]{:S(2)}) async-start(), calls=%async_computation.14 | async-start | bytes 10027008 | tf_op jit(solution)/shard_map/reduce_scatter | solution.py:186
  499.4 327.8 %all-gather.23.cloned.1.call-start = ((), (), s32[]{:S(2)}) async-start(), calls=%async_computation.11 | async-start | bytes 3760128 | tf_op jit(solution)/shard_map/all_gather | solution.py:122
  500.0 411.2 %all-reduce.26.cloned.1.call-start = ((), (), s32[]{:S(2)}) async-start(), calls=%async_computation.16 | async-start | bytes 3538944 | tf_op jit(solution)/shard_map/psum | solution.py:191
  778.1 60.8 %copy-start.19 = (f32[1176]{0:T(1024)S(1)}, f32[1176]{0:T(1024)}, u32[]{:S(2)}) copy-start(f32[1176]{0:T(1024)} %copy-done.18) | copy-start | bytes 14116
  838.9 3.7 copy-start.7
Sparse Core Ops, SparseCore 0:
  10.3 50.2 all-gather.8
  62.9 37.2 all-gather.10
  102.5 52.1 all-gather.12
  156.9 51.7 all-gather.14
  244.3 50.5 all-gather.16
  297.1 51.7 all-gather.18
  351.2 36.8 all-gather.20
  391.8 61.9 reduce-scatter.6
  458.5 110.3 reduce-scatter.10
  572.7 89.7 reduce-scatter.4
  667.1 110.8 reduce-scatter.8
  780.2 46.9 all-gather.22
  829.7 55.3 all-reduce.25
where the time goes:
time: 934 us; the launch traced here: 925 us
  waiting for transfers between devices  422 us (45%)
  matrix products  196 us (21%)
  blocking collectives  129 us (14%)
  local copies, waits for them, and re-layouts  119 us (13%)
  other arithmetic  41 us (4%)
  between operations  17.3 us (2%)
    unnamed x2, blocking collectives  123 us
    reduce_scatter x1, waiting for transfers between devices, local(): lax.psum_scatter(grad_up, 'fsdp', scatter_dimension=0, tiled=True)  116 us
    reduce_scatter x1, waiting for transfers between devices, local(): lax.psum_scatter(grad_attn_in, 'fsdp', scatter_dimension=0, tiled=True)  93.6 us
    reduce_scatter x1, waiting for transfers between devices, local(): lax.psum_scatter(grad_down, 'fsdp', scatter_dimension=0, tiled=True)  67.5 us
    all_gather x1, waiting for transfers between devices, local(): lax.all_gather(held[3], 'fsdp', axis=0, tiled=True)  49.4 us
    all_gather x1, waiting for transfers between devices, local(): lax.all_gather(held[0], 'fsdp', axis=0, tiled=True)  49.1 us
    dot_general x4, matrix products, outer_cols(): lax.dot_general(left, right, (((1,), (1,)), ((), ())), preferred_element_...  47.1 us
    unnamed x112, local copies, waits for them, and re-layouts  43.6 us
  transfers between devices with their start and end apart: 13, of which 7 were waited for; matrix products, arithmetic and copies ran while one was open for 36% of the time, Pallas kernels for 0%

commit v1 on v0

v1 whole, which is shorter than its diff:
```python
import functools
import math

import jax
import jax.numpy as jnp
from jax import lax
from jax.experimental import pallas as pl
from jax.experimental.pallas import tpu as pltpu
from jax.sharding import PartitionSpec as P

F32 = jnp.float32
BF16 = jnp.bfloat16
HEAD = 64
GROUP = 256
NEG = -1e30
VMEM = 56 * 2**20


def dot(a, b):
    return lax.dot_general(a, b, (((1,), (0,)), ((), ())), preferred_element_type=F32)


def dot_rows(a, b):
    return lax.dot_general(a, b, (((0,), (0,)), ((), ())), preferred_element_type=F32)


def dot_cols(a, b):
    return lax.dot_general(a, b, (((1,), (1,)), ((), ())), preferred_element_type=F32)


class Place:
    def __init__(self, count):
        self.count = count
        self.far = count // 4

    def own(self):
        index = lax.axis_index("fsdp")
        return index // 4, (index // 2) % 2, index % 2

    def other_core(self):
        return [(i, i ^ 1) for i in range(self.count)]

    def other_x(self):
        return [(i, i ^ 2) for i in range(self.count)]

    def along_z(self, step):
        return [(i, (i + 4 * step) % self.count) for i in range(self.count)]

    def row_of(self, own, dc, dx, dz):
        z, x, c = own
        zz = lax.rem(z + (dz % self.far), self.far)
        xx = x if dx == 0 else 1 - x
        cc = c if dc == 0 else 1 - c
        return (zz * 2 + xx) * 2 + cc


def gather_pieces(place, stack):
    came = [stack]
    for step in range(1, place.far):
        came.append(lax.ppermute(stack, "fsdp", place.along_z(step)))
    mine = jnp.stack(came)
    beside = lax.ppermute(mine, "fsdp", place.other_x())
    mine_core = lax.ppermute(mine, "fsdp", place.other_core())
    beside_core = lax.ppermute(beside, "fsdp", place.other_core())
    return [mine, beside, mine_core, beside_core]


def add_low(*terms):
    total = terms[0].astype(F32)
    for term in terms[1:]:
        total = total + term.astype(F32)
    return total


def scatter_pieces(place, keep, send):
    kind = keep.dtype
    came = lax.ppermute(send, "fsdp", place.other_core())
    across = add_low(keep[1], came[1]).astype(kind)
    from_x = lax.ppermute(across, "fsdp", place.other_x())
    parts = [add_low(keep[0, d], came[0, d], from_x[d]).astype(kind) for d in range(place.far)]
    terms = [parts[0]]
    for step in range(1, place.far):
        terms.append(lax.ppermute(parts[step], "fsdp", place.along_z(step)))
    summed = add_low(*terms).astype(kind)
    twin = lax.ppermute(summed, "rep", [(0, 1), (1, 0)])
    return add_low(summed, twin)


def load_weight(place, refs, spot, lead=0):
    own = place.own()
    rows = refs[0].shape[2]
    for which, ref in enumerate(refs):
        for d in range(place.far):
            at = place.row_of(own, which // 2, which % 2, -d) * rows
            spot[pl.ds(pl.multiple_of(at, 16), rows), :] = ref[d, lead]


def store_grad(place, spot, keep, send, lead=0):
    own = place.own()
    rows = keep.shape[3]
    for dc, ref in enumerate((keep, send)):
        for dx in range(2):
            for d in range(place.far):
                at = place.row_of(own, dc, dx, d) * rows
                ref[dx, d, lead] = spot[pl.ds(pl.multiple_of(at, 16), rows), :]


def norm_stats(v):
    mean = jnp.mean(v, axis=-1, keepdims=True)
    centred = v - mean
    spread = jnp.mean(centred * centred, axis=-1, keepdims=True)
    scale = lax.rsqrt(spread + 1e-06)
    return centred * scale, scale


def norm_back(up, xhat, scale, gain):
    e = up * gain
    return (e - jnp.mean(e, axis=-1, keepdims=True) - xhat * jnp.mean(e * xhat, axis=-1, keepdims=True)) * scale


ERF_P = 0.3275911 / math.sqrt(2.0)
ERF_A = (0.254829592, -0.284496736, 1.421413741, -1.453152027, 1.061405429)


def gelu_and_slope(z):
    t = 1.0 / (1.0 + ERF_P * jnp.abs(z))
    e = jnp.exp(-0.5 * (z * z))
    poly = 0.5 * ERF_A[4]
    for a in ERF_A[3::-1]:
        poly = poly * t + 0.5 * a
    q = poly * t * e
    phi = jnp.where(z > 0, 1.0 - q, q)
    return z * phi, phi + z * (e * (1.0 / math.sqrt(2.0 * math.pi)))


class Rows:
    def __init__(self, images, patches):
        self.images = images
        self.patches = patches
        self.pad = -(-patches // 16) * 16
        self.all = images * self.pad
        self.raw = images * patches


def flag_column(rows, flags):
    wide = flags[...].astype(F32)
    wide = jnp.concatenate([wide, jnp.zeros((8 - rows.images, rows.patches), F32)], axis=0)
    gap = -rows.patches % 128
    return jnp.concatenate([wide, jnp.zeros((8, gap), F32)], axis=1).T


def norm_one_kernel(rows, tokens, flags, grads, vec, base_o, norm_o, grad_o):
    cols = flag_column(rows, flags)
    token = vec[0:1, :]
    gain, shift = vec[1:2, :], vec[2:3, :]
    gap = jnp.zeros((rows.pad - rows.patches, tokens.shape[1]), F32)
    for i in range(rows.images):
        lo = rows.patches * i
        at = pl.ds(rows.pad * i, rows.pad)
        first = lo // 16 * 16
        last = min(-(-(lo + rows.patches) // 16) * 16, rows.raw)
        part = tokens[first:last, :].astype(F32)[lo - first : lo - first + rows.patches]
        base = jnp.where(cols[: rows.patches, i : i + 1] > 0.5, token, part)
        base = jnp.concatenate([base, gap], axis=0)
        base_o[at, :] = base.astype(BF16)
        xhat, _ = norm_stats(base)
        norm_o[at, :] = (xhat * gain + shift).astype(BF16)
        part = grads[first:last, :].astype(F32)[lo - first : lo - first + rows.patches]
        grad_o[at, :] = jnp.concatenate([part, gap], axis=0).astype(BF16)


def whole(shape):
    return pl.BlockSpec(shape, lambda *j: (0,) * len(shape))


def params():
    return pltpu.CompilerParams(vmem_limit_bytes=VMEM)


def cost(flops, count):
    return pl.CostEstimate(flops=int(flops), bytes_accessed=int(count), transcendentals=0)


def norm_one_call(rows, tokens, flags, grads, vec):
    width = tokens.shape[1]
    out = jax.ShapeDtypeStruct((rows.all, width), BF16)
    return pl.pallas_call(
        functools.partial(norm_one_kernel, rows),
        out_shape=[out, out, out],
        compiler_params=params(),
        cost_estimate=cost(4e9, 9e6),
        name="norm_one",
    )(tokens, flags, grads, vec)


def halves(x, first):
    zero = jnp.zeros_like(x)
    return jnp.concatenate([jnp.where(first, x, zero), jnp.where(first, zero, x)], axis=0)


def attend_kernel(place, rows, base_group, norm, vec, *refs):
    nw = 4 if place else 1
    w_in, (q_o, k_o, v_o, att_o, p_o), rest = refs[:nw], refs[nw : nw + 5], refs[nw + 5 :]
    j = pl.program_id(0)
    if place:
        w = rest[0].at[0]
        load_weight(place, w_in, w)
    else:
        w = w_in[0].at[0]
    x = norm[...]
    lanes = pl.ds(pl.multiple_of((base_group + j) * GROUP, GROUP), GROUP)
    q_o[0] = ((dot(x, w[:, 0:GROUP]) + vec[3:4, lanes]).astype(BF16) * 0.125).astype(BF16)
    k_o[0] = dot(x, w[:, GROUP : 2 * GROUP]).astype(BF16)
    v_o[0] = (dot(x, w[:, 2 * GROUP :]) + vec[4:5, lanes]).astype(BF16)
    s = rows.pad
    first = lax.broadcasted_iota(jnp.int32, (s, 128), 1) < HEAD
    live = lax.broadcasted_iota(jnp.int32, (s, 2 * s), 0) < rows.patches

    def image(i):
        at = pl.ds(pl.multiple_of(i * s, 16), s)
        for p in range(2):
            cols = pl.ds(128 * p, 128)
            q, k, v = q_o[0, at, cols], k_o[0, at, cols], v_o[0, at, cols]
            score = jnp.where(live, dot_cols(k, halves(q, first)), NEG)
            peak = jnp.max(score, axis=0, keepdims=True)
            e = jnp.exp(score - peak)
            probs = (e * (1.0 / jnp.sum(e, axis=0, keepdims=True))).astype(BF16)
            p_o[0, p, i] = probs
            o = dot_rows(probs, v)
            att_o[0, at, cols] = jnp.where(first, o[:s], o[s:]).astype(BF16)

    def step(i, carry):
        for u in range(3):
            image(i * 3 + u)
        return carry

    lax.fori_loop(0, rows.images // 3, step, 0)


def piece_specs(place, weight, blocks=1):
    if place is None:
        return [pl.BlockSpec((blocks, *weight[0].shape[1:]), lambda j: (j, 0, 0))]
    z, _, r, w = weight[0].shape
    return [pl.BlockSpec((z, blocks, r, w), lambda j: (0, j, 0, 0))] * 4


def attend_call(place, rows, base_group, groups, norm, vec, weight):
    s = rows.pad
    width = norm.shape[1]
    row = pl.BlockSpec((1, rows.all, GROUP), lambda j: (j, 0, 0))
    out = jax.ShapeDtypeStruct((groups, rows.all, GROUP), BF16)
    outs = [out] * 4 + [jax.ShapeDtypeStruct((groups, 2, rows.images, s, 2 * s), BF16)]
    specs = [row] * 4 + [pl.BlockSpec((1, 2, rows.images, s, 2 * s), lambda j: (j, 0, 0, 0, 0))]
    if place:
        outs.append(jax.ShapeDtypeStruct((groups, width, 3 * GROUP), BF16))
        specs.append(pl.BlockSpec((1, width, 3 * GROUP), lambda j: (j, 0, 0)))
    res = pl.pallas_call(
        functools.partial(attend_kernel, place, rows, base_group),
        grid=(groups,),
        in_specs=[whole(norm.shape), whole(vec.shape)] + piece_specs(place, weight),
        out_specs=specs,
        out_shape=outs,
        compiler_params=params(),
        cost_estimate=cost(groups * 6e9, groups * 8e6),
        name="attend",
    )(norm, vec, *weight)
    return list(res) if place else list(res) + [weight[0]]


def project_kernel(place, groups, vec, base, *refs):
    nw = 4 if place else 1
    na = len(groups)
    atts, w_in, rest = refs[:na], refs[na : na + nw], refs[na + nw :]
    resid_o, norm_o = rest[:2]
    if place:
        w = rest[2]
        load_weight(place, w_in, w)
    else:
        w = w_in[0].at[0]
    total = base[...].astype(F32) + vec[5:6, :]
    g = 0
    for a, count in zip(atts, groups):
        for b in range(count):
            total = total + dot(a[b], w[pl.ds(g * GROUP, GROUP), :])
            g += 1
    resid_o[...] = total
    xhat, _ = norm_stats(total)
    norm_o[...] = (xhat * vec[6:7, :] + vec[7:8, :]).astype(BF16)


def project_call(place, rows, vec, base, atts, weight):
    width = base.shape[1]
    outs = [jax.ShapeDtypeStruct((rows.all, width), F32), jax.ShapeDtypeStruct((rows.all, width), BF16)]
    if place:
        outs.append(jax.ShapeDtypeStruct((width, width), BF16))
    res = pl.pallas_call(
        functools.partial(project_kernel, place, [a.shape[0] for a in atts]),
        out_shape=outs,
        compiler_params=params(),
        cost_estimate=cost(3e9, 12e6),
        name="project",
    )(vec, base, *atts, *weight)
    return list(res) if place else list(res) + [weight[0][0]]


def feed_kernel(place, rows, first_block, carried, norm, grad, vec, *refs):
    nw = 4 if place else 1
    w_in, rest = refs[:nw], refs[nw:]
    if carried:
        (acc_in, gn_in), rest = rest[:2], rest[2:]
    acc_o, gn_o, bias_o = rest[:3]
    j = pl.program_id(0)
    if place:
        keep, send, w_up, w_down, act_s, gp_s, g_s = rest[3:]
        load_weight(place, w_in, w_up, 0)
        load_weight(place, w_in, w_down, 1)
    else:
        grads_o, act_s, gp_s = rest[3:]
        w_up, w_down = w_in[0].at[0], w_in[0].at[1]

    @pl.when(j == 0)
    def _():
        if carried:
            acc_o[...] = acc_in[...]
            gn_o[...] = gn_in[...]
        else:
            acc_o[...] = jnp.zeros_like(acc_o)
            gn_o[...] = jnp.zeros_like(gn_o)

    bias = vec[pl.ds(9 + first_block + j, 1), :]
    step = rows.pad
    for b in range(rows.images):
        at = pl.ds(b * step, step)
        z = dot(norm[at, :], w_up[...]) + bias
        up = dot_cols(grad[at, :], w_down[...])
        act, slope = gelu_and_slope(z)
        act = act.astype(BF16)
        gp = (up * slope).astype(BF16)
        act_s[at, :] = act
        gp_s[at, :] = gp
        acc_o[at, :] += dot(act, w_down[...])
        gn_o[at, :] += dot_cols(gp, w_up[...])
    bias_o[0] = jnp.sum(gp_s[...].astype(F32), axis=0, keepdims=True)
    g_up = dot_rows(norm[...], gp_s[...]).astype(BF16)
    if place:
        g_s[...] = g_up
        store_grad(place, g_s, keep, send, 0)
    else:
        grads_o[0] = g_up
    g_down = dot_rows(act_s[...], grad[...]).astype(BF16)
    if place:
        g_s[...] = g_down
        store_grad(place, g_s, keep, send, 1)
    else:
        grads_o[1] = g_down


def grad_out(place, blocks, width, r, per_step):
    if place is None:
        return (
            [jax.ShapeDtypeStruct((blocks, width, width), BF16)],
            [pl.BlockSpec((per_step, width, width), lambda j: (j, 0, 0))],
        )
    shape = (2, place.far, blocks, r, width)
    block = (2, place.far, per_step, r, width)
    return (
        [jax.ShapeDtypeStruct(shape, BF16)] * 2,
        [pl.BlockSpec(block, lambda j: (0, 0, j, 0, 0))] * 2,
    )


def feed_call(place, rows, first_block, blocks, norm, grad, vec, weight, carried=None):
    width = norm.shape[1]
    r = weight[0].shape[2] if place else None
    acc = jax.ShapeDtypeStruct((rows.all, width), F32)
    outs, specs = grad_out(place, 2 * blocks, width, r, 2)
    scratch = [pltpu.VMEM((rows.all, width), BF16)] * 2
    if place:
        scratch = [pltpu.VMEM((width, width), BF16)] * 2 + scratch + [pltpu.VMEM((width, width), BF16)]
    args = [norm, grad, vec, *weight]
    in_specs = [whole(norm.shape), whole(grad.shape), whole(vec.shape)] + piece_specs(place, weight, 2)
    if carried:
        args += list(carried)
        in_specs += [whole(acc.shape)] * 2
    return pl.pallas_call(
        functools.partial(feed_kernel, place, rows, first_block, bool(carried)),
        grid=(blocks,),
        in_specs=in_specs,
        out_specs=[whole(acc.shape)] * 2 + [pl.BlockSpec((1, 1, width), lambda j: (j, 0, 0))] + specs,
        out_shape=[acc, acc, jax.ShapeDtypeStruct((blocks, 1, width), F32)] + outs,
        scratch_shapes=scratch,
        compiler_params=params(),
        cost_estimate=cost(blocks * 1.2e10, blocks * 20e6),
        name="feed",
    )(*args)


def middle_kernel(rows, resid, acc, gn, grad, vec, w, out_o, gres_o, low_o, da_o, sums_o):
    xhat, scale = norm_stats(resid[...])
    gain = vec[6:7, :]
    up = gn[...]
    g = grad[...].astype(F32)
    total = g + norm_back(up, xhat, scale, gain)
    gres_o[...] = total
    low = total.astype(BF16)
    low_o[...] = low
    da_o[...] = dot_cols(low, w[...]).astype(BF16)
    sums_o[...] = jnp.concatenate(
        [
            jnp.sum(total, axis=0, keepdims=True),
            jnp.sum(up * xhat, axis=0, keepdims=True),
            jnp.sum(up, axis=0, keepdims=True),
            jnp.sum(g, axis=0, keepdims=True),
        ],
        axis=0,
    )
    final = resid[...] + acc[...] + vec[8:9, :]
    parts = [final[rows.pad * i : rows.pad * i + rows.patches] for i in range(rows.images)]
    out_o[...] = jnp.concatenate(parts, axis=0).astype(BF16)


def middle_call(rows, resid, acc, gn, grad, vec, w):
    width = resid.shape[1]
    return pl.pallas_call(
        functools.partial(middle_kernel, rows),
        out_shape=[
            jax.ShapeDtypeStruct((rows.raw, width), BF16),
            jax.ShapeDtypeStruct((rows.all, width), F32),
            jax.ShapeDtypeStruct((rows.all, width), BF16),
            jax.ShapeDtypeStruct((rows.all, width), BF16),
            jax.ShapeDtypeStruct((4, width), F32),
        ],
        compiler_params=params(),
        cost_estimate=cost(4e9, 20e6),
        name="middle",
    )(resid, acc, gn, grad, vec, w)


def attend_back_kernel(place, rows, base_group, projects, carried, norm, q_i, k_i, v_i, p_i, da, w, *refs):
    j = pl.program_id(0)
    lead = 1 if projects else 0
    if projects:
        (low, *atts), refs = refs[: 1 + projects], refs[1 + projects :]
    if carried:
        gn_in, refs = refs[0], refs[1:]
    gn_o, bias_o = refs[:2]
    if place:
        keep, send, d_s, g_s = refs[2:]
    else:
        grads_o, d_s = refs[2:]
    s = rows.pad
    first = lax.broadcasted_iota(jnp.int32, (s, 128), 1) < HEAD

    def emit(value):
        if place:
            g_s[...] = value.astype(BF16)
            store_grad(place, g_s, keep, send)
        else:
            grads_o[0] = value.astype(BF16)

    if projects:

        @pl.when(j == 0)
        def _():
            both = jnp.concatenate([a[b] for a in atts for b in range(a.shape[0])], axis=1)
            emit(dot_rows(both, low[...]))

    @pl.when(j == lead)
    def _():
        gn_o[...] = gn_in[...] if carried else jnp.zeros_like(gn_o)

    def image(i):
        at = pl.ds(pl.multiple_of(i * s, 16), s)
        for p in range(2):
            cols = pl.ds(128 * p, 128)
            q, k, v = q_i[0, at, cols], k_i[0, at, cols], v_i[0, at, cols]
            q2, da2 = halves(q, first), halves(da[at, cols], first)
            low_probs = p_i[0, p, i]
            d_s[at, pl.ds(2 * GROUP + 128 * p, 128)] = dot(low_probs, da2).astype(BF16)
            up = dot_cols(v, da2)
            probs = low_probs.astype(F32)
            inner = jnp.sum(probs * up, axis=0, keepdims=True)
            ds = (probs * (up - inner)).astype(BF16)
            d_s[at, pl.ds(GROUP + 128 * p, 128)] = dot(ds, q2).astype(BF16)
            dq = dot_rows(ds, k)
            d_s[at, cols] = (jnp.where(first, dq[:s], dq[s:]) * 0.125).astype(BF16)

    def group():
        def step(i, carry):
            for u in range(3):
                image(i * 3 + u)
            return carry

        lax.fori_loop(0, rows.images // 3, step, 0)
        bias_o[0] = jnp.sum(d_s[...].astype(F32), axis=0, keepdims=True)
        emit(dot_rows(norm[...], d_s[...]))
        gn_o[...] += dot_cols(d_s[...], w[0])

    if projects:
        pl.when(j >= 1)(group)
    else:
        group()


def attend_back_call(place, rows, base_group, norm, q, k, v, probs, da, w, r, project=None, carried=None):
    groups = q.shape[0]
    width = norm.shape[1]
    s = rows.pad
    lead = 1 if project else 0
    steps = groups + lead

    def at(j):
        return jnp.maximum(j - lead, 0) if lead else j

    row = pl.BlockSpec((1, rows.all, GROUP), lambda j: (at(j), 0, 0))
    in_specs = [whole(norm.shape), row, row, row]
    in_specs += [pl.BlockSpec((1, 2, rows.images, s, 2 * s), lambda j: (at(j), 0, 0, 0, 0))]
    in_specs += [pl.BlockSpec((rows.all, GROUP), lambda j: (0, base_group + at(j)))]
    in_specs += [pl.BlockSpec((1, width, 3 * GROUP), lambda j: (at(j), 0, 0))]
    args = [norm, q, k, v, probs, da, w]
    if project:
        args += list(project)
        in_specs += [whole(a.shape) for a in project]
    if carried is not None:
        args.append(carried)
        in_specs.append(whole(carried.shape))
    outs, specs = grad_out(place, steps, width, r, 1)
    scratch = [pltpu.VMEM((rows.all, 3 * GROUP), BF16)]
    if place:
        scratch.append(pltpu.VMEM((width, 3 * GROUP), BF16))
    return pl.pallas_call(
        functools.partial(
            attend_back_kernel, place, rows, base_group, len(project) - 1 if project else 0, carried is not None
        ),
        grid=(steps,),
        in_specs=in_specs,
        out_specs=[whole((rows.all, width)), pl.BlockSpec((1, 1, 3 * GROUP), lambda j: (at(j), 0, 0))] + specs,
        out_shape=[
            jax.ShapeDtypeStruct((rows.all, width), F32),
            jax.ShapeDtypeStruct((groups, 1, 3 * GROUP), F32),
        ]
        + outs,
        scratch_shapes=scratch,
        compiler_params=params(),
        cost_estimate=cost(steps * 8e9, steps * 12e6),
        name="attend_back",
    )(*args)


def last_kernel(rows, base, gn, gres, flags, vec, out_o, sums_o):
    cols = flag_column(rows, flags)
    gain = vec[1:2, :]
    token = jnp.zeros((1, base.shape[1]), F32)
    gain_sum, shift_sum = token, token
    for i in range(rows.images):
        at = pl.ds(rows.pad * i, rows.pad)
        xhat, scale = norm_stats(base[at, :].astype(F32))
        up = gn[at, :]
        total = gres[at, :] + norm_back(up, xhat, scale, gain)
        chosen = cols[: rows.pad, i : i + 1] > 0.5
        token = token + jnp.sum(jnp.where(chosen, total, 0.0), axis=0, keepdims=True)
        gain_sum = gain_sum + jnp.sum(up * xhat, axis=0, keepdims=True)
        shift_sum = shift_sum + jnp.sum(up, axis=0, keepdims=True)
        out_o[pl.ds(rows.patches * i, rows.patches), :] = jnp.where(chosen, 0.0, total)[: rows.patches]
    sums_o[...] = jnp.concatenate([token, gain_sum, shift_sum], axis=0)


def last_call(rows, base, gn, gres, flags, vec):
    width = base.shape[1]
    return pl.pallas_call(
        functools.partial(last_kernel, rows),
        out_shape=[jax.ShapeDtypeStruct((rows.raw, width), F32), jax.ShapeDtypeStruct((3, width), F32)],
        compiler_params=params(),
        cost_estimate=cost(4e9, 14e6),
        name="last",
    )(base, gn, gres, flags, vec)


def local(
    count,
    tokens,
    mask_flags,
    mask_token,
    norm1_gain,
    norm1_bias,
    qkv_weight,
    query_bias,
    value_bias,
    proj_weight,
    proj_bias,
    norm2_gain,
    norm2_bias,
    fc1_weight,
    fc1_bias,
    fc2_weight,
    fc2_bias,
    out_grad,
):
    images, patches = mask_flags.shape
    rows = Rows(images, patches)
    r, width = proj_weight.shape
    place = Place(count) if r % 16 == 0 else None
    quarter = fc1_weight.shape[1] // width

    qkv_blocks = qkv_weight.reshape(r, 3, 3, GROUP).transpose(2, 0, 1, 3).reshape(3, r, 3 * GROUP)
    up_blocks = fc1_weight.reshape(r, count, quarter, r).transpose(2, 0, 1, 3).reshape(quarter, r, width)
    down_blocks = fc2_weight.reshape(quarter, r, width)
    small = jnp.concatenate(
        [
            mask_token,
            norm1_gain,
            norm1_bias,
            query_bias,
            value_bias,
            proj_bias,
            norm2_gain,
            norm2_bias,
            fc2_bias,
            fc1_bias,
        ]
    )
    kinds = small.shape[0] // r

    if place:
        z, x, c = place.own()
        padded = jnp.pad(small, (0, -small.shape[0] % 1024)).reshape(1, -1, 128)
        came = jnp.stack(gather_pieces(place, padded))
        came = came.reshape(2, 2, place.far, -1)[..., : small.shape[0]]
        came = jnp.where(c == 0, came, came[::-1])
        came = jnp.where(x == 0, came, came[:, ::-1])
        came = jnp.roll(came[:, :, ::-1], z + 1, axis=2)
        came = came.transpose(2, 1, 0, 3).reshape(count, kinds, r)

        def gather(stack):
            return gather_pieces(place, stack)

        def scatter(pieces):
            return scatter_pieces(place, *pieces)

    else:
        came = lax.all_gather(small, "fsdp", axis=0, tiled=True).reshape(count, kinds, r)

        def gather(stack):
            return [lax.all_gather(stack, "fsdp", axis=1, tiled=True)]

        def scatter(pieces):
            share = lax.psum_scatter(pieces[0].astype(F32), "fsdp", scatter_dimension=1, tiled=True)
            return lax.psum(share, "rep")

    vec = came.transpose(1, 0, 2).reshape(kinds, width).astype(F32)
    vec = jnp.pad(vec, ((0, 16 - kinds), (0, 0)))

    w_a = gather(qkv_blocks[:1])
    w_b = gather(qkv_blocks[1:])
    w_p = gather(proj_weight[None])
    ff = jnp.stack([up_blocks, down_blocks], axis=1).reshape(2 * quarter, r, width)
    w_f = [gather(ff[:quarter]), gather(ff[quarter:])]

    base, norm, grad = norm_one_call(rows, tokens, mask_flags, out_grad, vec)
    q_a, k_a, v_a, att_a, p_a, wq_a = attend_call(place, rows, 0, 1, norm, vec, w_a)
    q_b, k_b, v_b, att_b, p_b, wq_b = attend_call(place, rows, 1, 2, norm, vec, w_b)
    resid, norm_two, w_proj = project_call(place, rows, vec, base, [att_a, att_b], w_p)

    half = quarter // 2
    acc, gn, gb_a, *gf_a = feed_call(place, rows, 0, half, norm_two, grad, vec, w_f[0])
    acc, gn, gb_b, *gf_b = feed_call(place, rows, half, half, norm_two, grad, vec, w_f[1], (acc, gn))
    sum_fa = scatter(gf_a)

    block_out, gres, low, da, sums_two = middle_call(rows, resid, acc, gn, grad, vec, w_proj)
    sum_fb = scatter(gf_b)
    gn1, qb_b, *gq_b = attend_back_call(
        place, rows, 1, norm, q_b, k_b, v_b, p_b, da, wq_b, r, project=[low, att_a, att_b]
    )
    sum_qb = scatter(gq_b)
    gn1, qb_a, *gq_a = attend_back_call(place, rows, 0, norm, q_a, k_a, v_a, p_a, da, wq_a, r, carried=gn1)
    sum_qa = scatter(gq_a)
    input_grad, sums_one = last_call(rows, base, gn1, gres, mask_flags, vec)

    qkv_sums = jnp.concatenate([qb_a, qb_b], axis=0)[:, 0]
    late = jnp.concatenate(
        [
            sums_one,
            qkv_sums[:, :GROUP].reshape(1, width),
            qkv_sums[:, 2 * GROUP :].reshape(1, width),
            sums_two,
            gb_a[:, 0],
            gb_b[:, 0],
        ],
        axis=0,
    )
    late = late.reshape(kinds, count, r).transpose(1, 0, 2).reshape(count, kinds * r)
    if place:
        late = jnp.pad(late, ((0, 0), (0, -late.shape[1] % 1024))).reshape(place.far, 2, 2, -1, 128)
        late = jnp.roll(late, -z, axis=0)
        late = jnp.where(x == 0, late, late[:, ::-1]).transpose(1, 2, 0, 3, 4)
        late = jnp.where(c == 0, late, late[:, ::-1])
        shares = scatter_pieces(place, late[:, 0], late[:, 1]).reshape(-1)[: kinds * r]
    else:
        shares = lax.psum(lax.psum_scatter(late, "fsdp", scatter_dimension=0, tiled=True), "rep").reshape(-1)
    shares = shares.reshape(kinds, r)
    token_s, gain1_s, shift1_s, qb_s, vb_s, pb_s, gain2_s, shift2_s, db_s = [shares[i] for i in range(9)]
    ub_s = shares[9:].reshape(-1)

    g_qkv = jnp.concatenate([sum_qa, sum_qb[1:]], axis=0).reshape(3, r, 3, GROUP)
    g_qkv = g_qkv.transpose(1, 2, 0, 3).reshape(r, 3 * width)
    g_ff = jnp.concatenate([sum_fa, sum_fb], axis=0).reshape(quarter, 2, r, width)
    g_up = g_ff[:, 0].reshape(quarter, r, count, r).transpose(1, 2, 0, 3).reshape(r, quarter * width)
    g_down = g_ff[:, 1].reshape(quarter * r, width)
    return (
        block_out,
        input_grad,
        token_s,
        gain1_s,
        shift1_s,
        g_qkv,
        qb_s,
        vb_s,
        sum_qb[0],
        pb_s,
        gain2_s,
        shift2_s,
        g_up,
        ub_s,
        g_down,
        db_s,
    )


def solution(mesh):
    both, one = P(("rep", "fsdp"), None), P("fsdp")
    flat = P("fsdp", None)
    in_specs = (both, both, one, one, one, flat, one, one, flat, one, one, one, flat, one, flat, one, both)
    out_specs = (both, both, one, one, one, flat, one, one, flat, one, one, one, flat, one, flat, one)
    return jax.shard_map(
        functools.partial(local, mesh.shape["fsdp"]),
        mesh=mesh,
        in_specs=in_specs,
        out_specs=out_specs,
        check_vma=False,
    )
```

time: 934 us -> 427 us (0.46)
  the two profiles are of different devices: /device:TPU:0 before, /device:TPU:10 now
where the time goes in v1:
time: 427 us; the launch traced here: 422 us
  Pallas kernels  158 us (37%)
  waiting for transfers between devices  147 us (34%)
  starting transfers between devices  82 us (19%)
  local copies, waits for them, and re-layouts  25.4 us (6%)
  other arithmetic  8.39 us (2%)
    pallas_call x2, Pallas kernels, feed_call(): pl.pallas_call(functools.partial(feed_kernel, place, rows, first_block, b...  59.8 us
    ppermute x18, waiting for transfers between devices, gather_pieces(): came.append(lax.ppermute(stack, 'fsdp', place.along_z(step)))  55.2 us
    pallas_call x2, Pallas kernels, attend_back_call(): pl.pallas_call(functools.partial(attend_back_kernel, place, rows, base_gr...  40.8 us
    ppermute x15, waiting for transfers between devices, scatter_pieces(): terms.append(lax.ppermute(parts[step], 'fsdp', place.along_z(step)))  32.8 us
    ppermute x15, starting transfers between devices, scatter_pieces(): terms.append(lax.ppermute(parts[step], 'fsdp', place.along_z(step)))  32.2 us
    ppermute x5, waiting for transfers between devices, scatter_pieces(): from_x = lax.ppermute(across, 'fsdp', place.other_x())  31.7 us
    ppermute x18, starting transfers between devices, gather_pieces(): came.append(lax.ppermute(stack, 'fsdp', place.along_z(step)))  24.5 us
    pallas_call x2, Pallas kernels, attend_call(): pl.pallas_call(functools.partial(attend_kernel, place, rows, base_group),...  21.8 us
  transfers between devices with their start and end apart: 66, of which 27 were waited for; matrix products, arithmetic and copies ran while one was open for 4% of the time, Pallas kernels for 37%

profile of v1, /device:TPU:10, one launch (start us, length us, event | category | flops | bytes accessed | tf_op | source)
XLA Modules:
  0.0 422.3 jit_solution(7111268405752216448)
XLA Ops:
  0.7 6.8 %concatenate.36 = bf16[624]{0:T(1024)(128)(2,1)S(1)} concatenate(bf16[48]{0:T(256)(128)(2,1)} %param.19, bf16[48]{0:T(256)(128)(2,1)} %param.20, bf16[48]{0:T(256)(128)(2,1)} %param.21, bf16[48]{0:T(256)(128)(2,1)} %param.23, bf16[48]{0:T(256)(128)(2,1)} %param.24, bf16[48]{0:T(256)(128)(2,1)} %param.26, bf16[48]{0:T(256)(128)(2,1)} %param.27, bf16[48]{0:T(256)(128)(2,1)} %param.28, ...), dimensions={0} | concatenate | bytes 2496 | tf_op jit(solution)/shard_map/concatenate | solution.py:608
  7.4 1.6 collective-permute-start
  10.3 1.8 collective-permute-start.2
  16.3 2.9 collective-permute-start.7
  20.6 1.7 reshape.449
  25.5 2.3 collective-permute-start.30
  28.1 2.1 collective-permute-start.13
  33.4 15.9 %collective-permute-done.19 = bf16[1,48,768]{2,1,0:T(8,128)(2,1)S(1)} collective-permute-done((bf16[1,48,768]{2,1,0:T(8,128)(2,1)S(1)}, bf16[1,48,768]{2,1,0:T(8,128)(2,1)S(1)}, u32[]{:S(2)}, u32[]{:S(2)}) %collective-permute-start.19) | collective-permute-done | bytes 73760 | tf_op jit(solution)/shard_map/ppermute | solution.py:60
  49.3 3.4 collective-permute-start.31
  53.1 1.7 collective-permute-start.24
  54.8 1.8 collective-permute-start.25
  56.6 1.5 collective-permute-start.9
  58.8 13.5 %collective-permute-done.31 = bf16[4,48,768]{2,1,0:T(8,128)(2,1)S(1)} collective-permute-done((bf16[4,48,768]{2,1,0:T(8,128)(2,1)S(1)}, bf16[4,48,768]{2,1,0:T(8,128)(2,1)S(1)}, u32[]{:S(2)}, u32[]{:S(2)}) %collective-permute-start.31) | collective-permute-done | bytes 294944 | tf_op jit(solution)/shard_map/ppermute | solution.py:60
  72.3 12.2 %collective-permute-done.32 = bf16[4,48,768]{2,1,0:T(8,128)(2,1)S(1)} collective-permute-done((bf16[4,48,768]{2,1,0:T(8,128)(2,1)S(1)}, bf16[4,48,768]{2,1,0:T(8,128)(2,1)S(1)}, u32[]{:S(2)}, u32[]{:S(2)}) %collective-permute-start.32) | collective-permute-done | bytes 294944 | tf_op jit(solution)/shard_map/ppermute | solution.py:60
  84.5 1.5 collective-permute-start.15
  86.1 6.2 %collective-permute-done.20 = bf16[1,48,768]{2,1,0:T(8,128)(2,1)S(1)} collective-permute-done((bf16[1,48,768]{2,1,0:T(8,128)(2,1)S(1)}, bf16[1,48,768]{2,1,0:T(8,128)(2,1)S(1)}, u32[]{:S(2)}, u32[]{:S(2)}) %collective-permute-start.20) | collective-permute-done | bytes 73760 | tf_op jit(solution)/shard_map/ppermute | solution.py:60
  92.6 5.3 %collective-permute-done.25 = bf16[4,48,768]{2,1,0:T(8,128)(2,1)S(1)} collective-permute-done((bf16[4,48,768]{2,1,0:T(8,128)(2,1)S(1)}, bf16[4,48,768]{2,1,0:T(8,128)(2,1)S(1)}, u32[]{:S(2)}, u32[]{:S(2)}) %collective-permute-start.25) | collective-permute-done | bytes 294944 | tf_op jit(solution)/shard_map/ppermute | solution.py:60
  97.9 1.5 collective-permute-start.33
  99.4 6.5 %norm_one.1 = (bf16[1248,768]{1,0:T(8,128)(2,1)}, bf16[1248,768]{1,0:T(8,128)(2,1)}, bf16[1248,768]{1,0:T(8,128)(2,1)}) custom-call(bf16[1176,768]{1,0:T(8,128)(2,1)} %tokens.1, s32[6,196]{1,0:T(8,128)} %flags.3, bf16[1176,768]{1,0:T(8,128)(2,1)} %grads.1, f32[16,768]{1,0:T(8,128)} %pad_convert_fusion.vec), custom_call_target="tpu_custom_call" | custom-call | flops 4000000000 | bytes 9000000 | tf_op jit(solution)/shard_map/norm_one/pallas_call | solution.py:187
  108.1 8.3 %attend.2 = (bf16[1,1248,256]{2,1,0:T(8,128)(2,1)}, bf16[1,1248,256]{2,1,0:T(8,128)(2,1)}, bf16[1,1248,256]{2,1,0:T(8,128)(2,1)}, bf16[1,1248,256]{2,1,0:T(8,128...) custom-call(bf16[1248,768]{1,0:T(8,128)(2,1)} %get-tuple-element.60.norm, ...), custom_call_target="tpu_custom_call" | custom-call | flops 6000000000 | bytes 8000000 | tf_op jit(solution)/shard_map/attend/pallas_call | solution.py:257
  116.4 14.9 %collective-permute-done.21.refs_3_ = bf16[4,1,48,768]{3,2,1,0:T(8,128)(2,1)S(1)} collective-permute-done((bf16[4,1,48,768]{3,2,1,0:T(8,128)(2,1)S(1)}, bf16[4,1,48,768]{3,2,1,0:T(8,128)(2,1)S(1)}, u32[]{:S(2)}, u32[]{:S(2)}) %collective-permute-start.21) | collective-permute-done | bytes 294944 | tf_op jit(solution)/shard_map/ppermute | solution.py:62
  131.3 1.6 collective-permute-start.27
  133.3 13.4 %attend.3 = (bf16[2,1248,256]{2,1,0:T(8,128)(2,1)}, bf16[2,1248,256]{2,1,0:T(8,128)(2,1)}, bf16[2,1248,256]{2,1,0:T(8,128)(2,1)}, bf16[2,1248,256]{2,1,0:T(8,128...) custom-call(bf16[1248,768]{1,0:T(8,128)(2,1)} %get-tuple-element.60.norm, ...), custom_call_target="tpu_custom_call" | custom-call | flops 12000000000 | bytes 16000000 | tf_op jit(solution)/shard_map/attend/pallas_call | solution.py:257
  148.0 7.6 %project.1 = (f32[1248,768]{1,0:T(8,128)}, bf16[1248,768]{1,0:T(8,128)(2,1)}, bf16[768,768]{1,0:T(8,128)(2,1)}) custom-call(f32[16,768]{1,0:T(8,128)} %pad_convert_fusion.vec, bf16[1248,768]{1,0:T(8,128)(2,1)} %get-tuple-element.59.base, bf16[1,1248,256]{2,1,0:T(8,128)(2,1)} %get-tuple-element.61.refs_0_.refs_1_, ...), custom_call_target="tpu_custom_call" | custom-call | flops 3000000000 | bytes 12000000 | tf_op jit(solution)/shard_map/project/pallas_call | solution.py:296
  155.6 4.1 collective-permute-done.27.refs_1_
  161.1 28.6 %feed.2 = (f32[1248,768]{1,0:T(8,128)}, f32[1248,768]{1,0:T(8,128)}, f32[2,1,768]{2,1,0:T(1,128)}, bf16[2,4,4,48,768]{4,3,2,1,0:T(8,128)(2,1)}, bf16[2,4,4,48,768]{4,3,2,1,0:T(8,128)(2,1)}) custom-call(bf16[1248,768]{1,0:T(8,128)(2,1)} %get-tuple-element.64.norm, bf16[1248,768]{1,0:T(8,128)(2,1)} %get-tuple-element.65.grad, f32[16,768]{1,0:T(8,128)} %pad_convert_fusion.vec, ...), custom_call_target="tpu_custom_call" | custom-call | flops 24000000000 | bytes 40000000 | tf_op jit(solution)/shard_map/feed/pallas_call | solution.py:385
  190.3 31.2 %feed.3 = (f32[1248,768]{1,0:T(8,128)}, f32[1248,768]{1,0:T(8,128)}, f32[2,1,768]{2,1,0:T(1,128)}, bf16[2,4,4,48,768]{4,3,2,1,0:T(8,128)(2,1)}, bf16[2,4,4,48,768]{4,3,2,1,0:T(8,128)(2,1)}) custom-call(bf16[1248,768]{1,0:T(8,128)(2,1)} %get-tuple-element.64.norm, bf16[1248,768]{1,0:T(8,128)(2,1)} %get-tuple-element.65.grad, f32[16,768]{1,0:T(8,128)} %pad_convert_fusion.vec, ...), custom_call_target="tpu_custom_call" | custom-call | flops 24000000000 | bytes 40000000 | tf_op jit(solution)/shard_map/feed/pallas_call | solution.py:385
  221.5 12.1 %middle.1 = (bf16[1176,768]{1,0:T(8,128)(2,1)}, f32[1248,768]{1,0:T(8,128)}, bf16[1248,768]{1,0:T(8,128)(2,1)}, bf16[1248,768]{1,0:T(8,128)(2,1)}, f32[4,768]{1,0:T(4,128)}) custom-call(f32[1248,768]{1,0:T(8,128)} %get-tuple-element.63.resid, f32[1248,768]{1,0:T(8,128)} %get-tuple-element.68.acc, f32[1248,768]{1,0:T(8,128)} %get-tuple-element.69.gn, ...), custom_call_target="tpu_custom_call" | custom-call | flops 4000000000 | bytes 20000000 | tf_op jit(solution)/shard_map/middle/pallas_call | solution.py:424
  233.6 25.5 %attend_back.2 = (f32[1248,768]{1,0:T(8,128)}, f32[2,1,768]{2,1,0:T(1,128)}, bf16[2,4,3,48,768]{4,3,2,1,0:T(8,128)(2,1)}, bf16[2,4,3,48,768]{4,3,2,1,0:T(8,128)(2,1)}) custom-call(bf16[1248,768]{1,0:T(8,128)(2,1)} %get-tuple-element.60.norm, bf16[2,1248,256]{2,1,0:T(8,128)(2,1)} %get-tuple-element.78.q_i, bf16[2,1248,256]{2,1,0:T(8,128)(2,1)} %get-tuple-element.79.k_i, ...), custom_call_target="tpu_custom_call" | custom-call | flops 24000000000 | bytes 36000000 | tf_op jit(solution)/shard_map/attend_back/pallas_call | solution.py:531
  259.2 15.3 %attend_back.3 = (f32[1248,768]{1,0:T(8,128)}, f32[1,1,768]{2,1,0:T(1,128)}, bf16[2,4,1,48,768]{4,3,2,1,0:T(8,128)(2,1)}, bf16[2,4,1,48,768]{4,3,2,1,0:T(8,128)(2,1)}) custom-call(bf16[1248,768]{1,0:T(8,128)(2,1)} %get-tuple-element.60.norm, bf16[1,1248,256]{2,1,0:T(8,128)(2,1)} %get-tuple-element.72.q_i, bf16[1,1248,256]{2,1,0:T(8,128)(2,1)} %get-tuple-element.73.k_i, ...), custom_call_target="tpu_custom_call" | custom-call | flops 8000000000 | bytes 12000000 | tf_op jit(solution)/shard_map/attend_back/pallas_call | solution.py:531
  275.4 9.1 %last.1 = (f32[1176,768]{1,0:T(8,128)}, f32[3,768]{1,0:T(4,128)}) custom-call(bf16[1248,768]{1,0:T(8,128)(2,1)} %get-tuple-element.59.base, f32[1248,768]{1,0:T(8,128)} %get-tuple-element.85.gn, f32[1248,768]{1,0:T(8,128)} %get-tuple-element.86.gres, s32[6,196]{1,0:T(8,128)} %flags.3, f32[16,768]{1,0:T(8,128)} %pad_convert_fusion.vec), custom_call_target="tpu_custom_call" | custom-call | flops 4000000000 | bytes 14000000 | tf_op jit(solution)/shard_map/last/pallas_call | solution.py:570
  289.2 2.2 collective-permute-done.37
  291.4 3.6 collective-permute-done.38
  295.0 3.3 collective-permute-start.39
  298.3 1.6 collective-permute-done.39
  299.8 2.4 collective-permute-start.40
  303.5 1.5 collective-permute-start.41
  305.1 2.1 collective-permute-done.41
  307.2 1.6 collective-permute-start.43
  310.0 1.5 fusion.2
  312.2 5.1 %collective-permute-done.43 = bf16[4,1,48,768]{3,2,1,0:T(8,128)(2,1)S(1)} collective-permute-done((bf16[4,1,48,768]{3,2,1,0:T(8,128)(2,1)S(1)}, bf16[4,1,48,768]{3,2,1,0:T(8,128)(2,1)S(1)}, u32[]{:S(2)}, u32[]{:S(2)}) %collective-permute-start.43) | collective-permute-done | bytes 294944 | tf_op jit(solution)/shard_map/ppermute | solution.py:79
  318.8 3.3 collective-permute-start.45
  322.1 2.2 collective-permute-start.46
  324.6 1.6 collective-permute-start.55
  326.8 1.6 collective-permute-start.47
  328.7 1.5 collective-permute-start.61
  330.3 5.9 %collective-permute-done.49 = bf16[4,3,48,768]{3,2,1,0:T(8,128)(2,1)S(1)} collective-permute-done((bf16[4,3,48,768]{3,2,1,0:T(8,128)(2,1)S(1)}, bf16[4,3,48,768]{3,2,1,0:T(8,128)(2,1)S(1)}, u32[]{:S(2)}, u32[]{:S(2)}) %collective-permute-start.49) | collective-permute-done | bytes 884768 | tf_op jit(solution)/shard_map/ppermute | solution.py:79
  339.0 3.3 collective-permute-start.51
  342.4 1.9 collective-permute-start.52
  344.4 6.3 %collective-permute-done.51 = bf16[3,48,768]{2,1,0:T(8,128)(2,1)S(1)} collective-permute-done((bf16[3,48,768]{2,1,0:T(8,128)(2,1)S(1)}, bf16[3,48,768]{2,1,0:T(8,128)(2,1)S(1)}, u32[]{:S(2)}, u32[]{:S(2)}) %collective-permute-start.51) | collective-permute-done | bytes 221216 | tf_op jit(solution)/shard_map/ppermute | solution.py:83
  350.6 2.8 collective-permute-done.52
  354.5 1.6 collective-permute-start.53
  356.1 5.4 %collective-permute-done.55 = bf16[4,4,48,768]{3,2,1,0:T(8,128)(2,1)S(1)} collective-permute-done((bf16[4,4,48,768]{3,2,1,0:T(8,128)(2,1)S(1)}, bf16[4,4,48,768]{3,2,1,0:T(8,128)(2,1)S(1)}, u32[]{:S(2)}, u32[]{:S(2)}) %collective-permute-start.55) | collective-permute-done | bytes 1179680 | tf_op jit(solution)/shard_map/ppermute | solution.py:79
  363.3 3.4 collective-permute-start.57
  366.7 2.0 collective-permute-start.58
  368.7 13.2 %collective-permute-done.61 = bf16[4,4,48,768]{3,2,1,0:T(8,128)(2,1)S(1)} collective-permute-done((bf16[4,4,48,768]{3,2,1,0:T(8,128)(2,1)S(1)}, bf16[4,4,48,768]{3,2,1,0:T(8,128)(2,1)S(1)}, u32[]{:S(2)}, u32[]{:S(2)}) %collective-permute-start.61) | collective-permute-done | bytes 1179680 | tf_op jit(solution)/shard_map/ppermute | solution.py:79
  383.5 3.3 collective-permute-start.63
  389.2 1.6 collective-permute-start.59
  390.8 10.1 %collective-permute-done.62 = bf16[4,48,768]{2,1,0:T(8,128)(2,1)S(1)} collective-permute-done((bf16[4,48,768]{2,1,0:T(8,128)(2,1)S(1)}, bf16[4,48,768]{2,1,0:T(8,128)(2,1)S(1)}, u32[]{:S(2)}, u32[]{:S(2)}) %collective-permute-start.62) | collective-permute-done | bytes 294944 | tf_op jit(solution)/shard_map/ppermute | solution.py:83
  401.0 3.2 collective-permute-done.63
  404.1 3.4 collective-permute-done.64
  407.8 1.6 collective-permute-start.65
  411.1 5.2 %collective-permute-done.65 = bf16[4,48,768]{2,1,0:T(8,128)(2,1)S(1)} collective-permute-done((bf16[4,48,768]{2,1,0:T(8,128)(2,1)S(1)}, bf16[4,48,768]{2,1,0:T(8,128)(2,1)S(1)}, u32[]{:S(2)}, u32[]{:S(2)}) %collective-permute-start.65) | collective-permute-done | bytes 294944 | tf_op jit(solution)/shard_map/ppermute | solution.py:85
  419.2 2.6 reshape.456
  (223 shorter events, 46.7 us)
Async XLA Ops:
  7.4 5.7 %collective-permute-start = (bf16[1,8,128]{2,1,0:T(8,128)(2,1)S(1)}, bf16[1,8,128]{2,1,0:T(8,128)(2,1)S(1)}, u32[]{:S(2)}, u32[]{:S(2)}) collective-permute-start(bf16[1,8,128]{2,1,0:T(8,128)(2,1)S(1)} %get-tuple-element.137), channel_id=1, source_target_pairs={{0,4},{1,5},{2,6},{3,7},{4,8},{5,9},{6,10},{7,11},{8,12},{9,13},{1... | collective-permute-start | bytes 6152 | tf_op jit(solution)/shard_map/ppermute | solution.py:60
  9.0 4.5 %collective-permute-start.1 = (bf16[1,8,128]{2,1,0:T(8,128)(2,1)S(1)}, bf16[1,8,128]{2,1,0:T(8,128)(2,1)S(1)}, u32[]{:S(2)}, u32[]{:S(2)}) collective-permute-start(bf16[1,8,128]{2,1,0:T(8,128)(2,1)S(1)} %get-tuple-element.137), channel_id=1, source_target_pairs={{0,8},{1,9},{2,10},{3,11},{4,12},{5,13},{6,14},{7,15},{8,0},{9,1},... | collective-permute-start | bytes 6152 | tf_op jit(solution)/shard_map/ppermute | solution.py:60
  10.3 3.6 collective-permute-start.2
  13.9 9.4 %collective-permute-start.3 = (bf16[4,1,8,128]{3,2,0,1:T(8,128)(2,1)S(1)}, bf16[4,1,8,128]{3,2,0,1:T(8,128)(2,1)S(1)}, u32[]{:S(2)}, u32[]{:S(2)}) collective-permute-start(bf16[4,1,8,128]{3,2,0,1:T(8,128)(2,1)S(1)} %get-tuple-element.126), channel_id=1, source_target_pairs={{0,2},{1,3},{2,0},{3,1},{4,6},{5,7},{6,4},{7,5},{8,10},{9,11},{10,... | collective-permute-start | bytes 24584 | tf_op jit(solution)/shard_map/ppermute | solution.py:62
  14.9 10.7 %collective-permute-start.6 = (bf16[1,48,768]{2,1,0:T(8,128)(2,1)S(1)}, bf16[1,48,768]{2,1,0:T(8,128)(2,1)S(1)}, u32[]{:S(2)}, u32[]{:S(2)}) collective-permute-start(bf16[1,48,768]{2,1,0:T(8,128)(2,1)S(1)} %slice.316), channel_id=1, source_target_pairs={{0,4},{1,5},{2,6},{3,7},{4,8},{5,9},{6,10},{7,11},{8,12},{9,13},{1... | collective-permute-start | bytes 221192 | tf_op jit(solution)/shard_map/ppermute | solution.py:60
  16.3 11.8 %collective-permute-start.7 = (bf16[1,48,768]{2,1,0:T(8,128)(2,1)S(1)}, bf16[1,48,768]{2,1,0:T(8,128)(2,1)S(1)}, u32[]{:S(2)}, u32[]{:S(2)}) collective-permute-start(bf16[1,48,768]{2,1,0:T(8,128)(2,1)S(1)} %slice.316), channel_id=1, source_target_pairs={{0,8},{1,9},{2,10},{3,11},{4,12},{5,13},{6,14},{7,15},{8,0},{9,1},... | collective-permute-start | bytes 221192 | tf_op jit(solution)/shard_map/ppermute | solution.py:60
  19.2 11.0 %collective-permute-start.8 = (bf16[1,48,768]{2,1,0:T(8,128)(2,1)S(1)}, bf16[1,48,768]{2,1,0:T(8,128)(2,1)S(1)}, u32[]{:S(2)}, u32[]{:S(2)}) collective-permute-start(bf16[1,48,768]{2,1,0:T(8,128)(2,1)S(1)} %slice.316), channel_id=1, source_target_pairs={{0,12},{1,13},{2,14},{3,15},{4,0},{5,1},{6,2},{7,3},{8,4},{9,5},{1... | collective-permute-start | bytes 221192 | tf_op jit(solution)/shard_map/ppermute | solution.py:60
  23.3 2.1 collective-permute-start.5
  24.6 28.0 %collective-permute-start.12 = (bf16[2,48,768]{2,1,0:T(8,128)(2,1)S(1)}, bf16[2,48,768]{2,1,0:T(8,128)(2,1)S(1)}, u32[]{:S(2)}, u32[]{:S(2)}) collective-permute-start(bf16[2,48,768]{2,1,0:T(8,128)(2,1)S(1)} %slice.318), channel_id=1, source_target_pairs={{0,4},{1,5},{2,6},{3,7},{4,8},{5,9},{6,10},{7,11},{8,12},{9,13},{1... | collective-permute-start | bytes 442376 | tf_op jit(solution)/shard_map/ppermute | solution.py:60
  25.4 7.6 %collective-permute-start.18 = (bf16[1,48,768]{2,1,0:T(8,128)(2,1)S(1)}, bf16[1,48,768]{2,1,0:T(8,128)(2,1)S(1)}, u32[]{:S(2)}, u32[]{:S(2)}) collective-permute-start(bf16[1,48,768]{2,1,0:T(8,128)(2,1)S(1)} %bitcast.293), channel_id=1, source_target_pairs={{0,4},{1,5},{2,6},{3,7},{4,8},{5,9},{6,10},{7,11},{8,12},{9,13},{1... | collective-permute-start | bytes 221192 | tf_op jit(solution)/shard_map/ppermute | solution.py:60
  25.5 31.1 %collective-permute-start.30 = (bf16[4,48,768]{2,1,0:T(8,128)(2,1)S(1)}, bf16[4,48,768]{2,1,0:T(8,128)(2,1)S(1)}, u32[]{:S(2)}, u32[]{:S(2)}) collective-permute-start(bf16[4,48,768]{2,1,0:T(8,128)(2,1)S(1)} %bitcast.271), channel_id=1, source_target_pairs={{0,4},{1,5},{2,6},{3,7},{4,8},{5,9},{6,10},{7,11},{8,12},{9,13},{1... | collective-permute-start | bytes 884744 | tf_op jit(solution)/shard_map/ppermute | solution.py:60
  28.1 25.0 %collective-permute-start.13 = (bf16[2,48,768]{2,1,0:T(8,128)(2,1)S(1)}, bf16[2,48,768]{2,1,0:T(8,128)(2,1)S(1)}, u32[]{:S(2)}, u32[]{:S(2)}) collective-permute-start(bf16[2,48,768]{2,1,0:T(8,128)(2,1)S(1)} %slice.318), channel_id=1, source_target_pairs={{0,8},{1,9},{2,10},{3,11},{4,12},{5,13},{6,14},{7,15},{8,0},{9,1},... | collective-permute-start | bytes 442376 | tf_op jit(solution)/shard_map/ppermute | solution.py:60
  30.2 24.6 %collective-permute-start.14 = (bf16[2,48,768]{2,1,0:T(8,128)(2,1)S(1)}, bf16[2,48,768]{2,1,0:T(8,128)(2,1)S(1)}, u32[]{:S(2)}, u32[]{:S(2)}) collective-permute-start(bf16[2,48,768]{2,1,0:T(8,128)(2,1)S(1)} %slice.318), channel_id=1, source_target_pairs={{0,12},{1,13},{2,14},{3,15},{4,0},{5,1},{6,2},{7,3},{8,4},{9,5},{1... | collective-permute-start | bytes 442376 | tf_op jit(solution)/shard_map/ppermute | solution.py:60
  33.0 16.3 %collective-permute-start.19 = (bf16[1,48,768]{2,1,0:T(8,128)(2,1)S(1)}, bf16[1,48,768]{2,1,0:T(8,128)(2,1)S(1)}, u32[]{:S(2)}, u32[]{:S(2)}) collective-permute-start(bf16[1,48,768]{2,1,0:T(8,128)(2,1)S(1)} %bitcast.294), channel_id=1, source_target_pairs={{0,8},{1,9},{2,10},{3,11},{4,12},{5,13},{6,14},{7,15},{8,0},{9,1},... | collective-permute-start | bytes 221192 | tf_op jit(solution)/shard_map/ppermute | solution.py:60
  49.3 23.0 %collective-permute-start.31 = (bf16[4,48,768]{2,1,0:T(8,128)(2,1)S(1)}, bf16[4,48,768]{2,1,0:T(8,128)(2,1)S(1)}, u32[]{:S(2)}, u32[]{:S(2)}) collective-permute-start(bf16[4,48,768]{2,1,0:T(8,128)(2,1)S(1)} %bitcast.272), channel_id=1, source_target_pairs={{0,8},{1,9},{2,10},{3,11},{4,12},{5,13},{6,14},{7,15},{8,0},{9,1},... | collective-permute-start | bytes 884744 | tf_op jit(solution)/shard_map/ppermute | solution.py:60
  52.7 31.8 %collective-permute-start.32 = (bf16[4,48,768]{2,1,0:T(8,128)(2,1)S(1)}, bf16[4,48,768]{2,1,0:T(8,128)(2,1)S(1)}, u32[]{:S(2)}, u32[]{:S(2)}) collective-permute-start(bf16[4,48,768]{2,1,0:T(8,128)(2,1)S(1)} %bitcast.273), channel_id=1, source_target_pairs={{0,12},{1,13},{2,14},{3,15},{4,0},{5,1},{6,2},{7,3},{8,4},{9,5},{1... | collective-permute-start | bytes 884744 | tf_op jit(solution)/shard_map/ppermute | solution.py:60
  53.1 39.3 %collective-permute-start.24 = (bf16[4,48,768]{2,1,0:T(8,128)(2,1)S(1)}, bf16[4,48,768]{2,1,0:T(8,128)(2,1)S(1)}, u32[]{:S(2)}, u32[]{:S(2)}) collective-permute-start(bf16[4,48,768]{2,1,0:T(8,128)(2,1)S(1)} %bitcast.267), channel_id=1, source_target_pairs={{0,4},{1,5},{2,6},{3,7},{4,8},{5,9},{6,10},{7,11},{8,12},{9,13},{1... | collective-permute-start | bytes 884744 | tf_op jit(solution)/shard_map/ppermute | solution.py:60
  54.8 43.1 %collective-permute-start.25 = (bf16[4,48,768]{2,1,0:T(8,128)(2,1)S(1)}, bf16[4,48,768]{2,1,0:T(8,128)(2,1)S(1)}, u32[]{:S(2)}, u32[]{:S(2)}) collective-permute-start(bf16[4,48,768]{2,1,0:T(8,128)(2,1)S(1)} %bitcast.268), channel_id=1, source_target_pairs={{0,8},{1,9},{2,10},{3,11},{4,12},{5,13},{6,14},{7,15},{8,0},{9,1},... | collective-permute-start | bytes 884744 | tf_op jit(solution)/shard_map/ppermute | solution.py:60
  56.6 42.8 %collective-permute-start.9 = (bf16[4,1,48,768]{3,2,1,0:T(8,128)(2,1)S(1)}, bf16[4,1,48,768]{3,2,1,0:T(8,128)(2,1)S(1)}, u32[]{:S(2)}, u32[]{:S(2)}) collective-permute-start(bf16[4,1,48,768]{3,2,1,0:T(8,128)(2,1)S(1)} %pad_maximum_fusion.6.refs_0_), channel_id=1, source_target_pairs={{0,2},{1,3},{2,0},{3,1},{4,6},{5,7},{6,4},{7,5},{8,10},{9,11},{10,... | collective-permute-start | bytes 884744 | tf_op jit(solution)/shard_map/ppermute | solution.py:62
  72.3 20.0 %collective-permute-start.20 = (bf16[1,48,768]{2,1,0:T(8,128)(2,1)S(1)}, bf16[1,48,768]{2,1,0:T(8,128)(2,1)S(1)}, u32[]{:S(2)}, u32[]{:S(2)}) collective-permute-start(bf16[1,48,768]{2,1,0:T(8,128)(2,1)S(1)} %bitcast.295), channel_id=1, source_target_pairs={{0,12},{1,13},{2,14},{3,15},{4,0},{5,1},{6,2},{7,3},{8,4},{9,5},{1... | collective-permute-start | bytes 221192 | tf_op jit(solution)/shard_map/ppermute | solution.py:60
  84.5 21.9 %collective-permute-start.15 = (bf16[4,2,48,768]{3,2,1,0:T(8,128)(2,1)S(1)}, bf16[4,2,48,768]{3,2,1,0:T(8,128)(2,1)S(1)}, u32[]{:S(2)}, u32[]{:S(2)}) collective-permute-start(bf16[4,2,48,768]{3,2,1,0:T(8,128)(2,1)S(1)} %pad_maximum_fusion.3.refs_0_), channel_id=1, source_target_pairs={{0,2},{1,3},{2,0},{3,1},{4,6},{5,7},{6,4},{7,5},{8,10},{9,11},{10,... | collective-permute-start | bytes 1769480 | tf_op jit(solution)/shard_map/ppermute | solution.py:62
  92.3 13.6 %collective-permute-start.26 = (bf16[4,48,768]{2,1,0:T(8,128)(2,1)S(1)}, bf16[4,48,768]{2,1,0:T(8,128)(2,1)S(1)}, u32[]{:S(2)}, u32[]{:S(2)}) collective-permute-start(bf16[4,48,768]{2,1,0:T(8,128)(2,1)S(1)} %bitcast.269), channel_id=1, source_target_pairs={{0,12},{1,13},{2,14},{3,15},{4,0},{5,1},{6,2},{7,3},{8,4},{9,5},{1... | collective-permute-start | bytes 884744 | tf_op jit(solution)/shard_map/ppermute | solution.py:60
  92.5 14.2 %collective-permute-start.10 = (bf16[4,1,48,768]{3,2,1,0:T(8,128)(2,1)S(1)}, bf16[4,1,48,768]{3,2,1,0:T(8,128)(2,1)S(1)}, u32[]{:S(2)}, u32[]{:S(2)}) collective-permute-start(bf16[4,1,48,768]{3,2,1,0:T(8,128)(2,1)S(1)} %pad_maximum_fusion.6.refs_0_), channel_id=1, source_target_pairs={{0,1},{1,0},{2,3},{3,2},{4,5},{5,4},{6,7},{7,6},{8,9},{9,8},{10,11... | collective-permute-start | bytes 884744 | tf_op jit(solution)/shard_map/ppermute | solution.py:63
  97.9 35.1 %collective-permute-start.33 = (bf16[4,4,48,768]{3,2,1,0:T(8,128)(2,1)S(1)}, bf16[4,4,48,768]{3,2,1,0:T(8,128)(2,1)S(1)}, u32[]{:S(2)}, u32[]{:S(2)}) collective-permute-start(bf16[4,4,48,768]{3,2,1,0:T(8,128)(2,1)S(1)} %pad_maximum_fusion.1.refs_0_), channel_id=1, source_target_pairs={{0,2},{1,3},{2,0},{3,1},{4,6},{5,7},{6,4},{7,5},{8,10},{9,11},{10,... | collective-permute-start | bytes 3538952 | tf_op jit(solution)/shard_map/ppermute | solution.py:62
  99.4 8.0 %collective-permute-start.11 = (bf16[4,1,48,768]{3,2,1,0:T(8,128)(2,1)S(1)}, bf16[4,1,48,768]{3,2,1,0:T(8,128)(2,1)S(1)}, u32[]{:S(2)}, u32[]{:S(2)}) collective-permute-start(bf16[4,1,48,768]{3,2,1,0:T(8,128)(2,1)S(1)} %collective-permute-done.9.refs_1_), channel_id=1, source_target_pairs={{0,1},{1,0},{2,3},{3,2},{4,5},{5,4},{6,7},{7,6},{8,9},{9,8},{10,11... | collective-permute-start | bytes 884744 | tf_op jit(solution)/shard_map/ppermute | solution.py:64
  105.9 25.3 %collective-permute-start.16 = (bf16[4,2,48,768]{3,2,1,0:T(8,128)(2,1)S(1)}, bf16[4,2,48,768]{3,2,1,0:T(8,128)(2,1)}, u32[]{:S(2)}, u32[]{:S(2)}) collective-permute-start(bf16[4,2,48,768]{3,2,1,0:T(8,128)(2,1)S(1)} %pad_maximum_fusion.3.refs_0_), channel_id=1, source_target_pairs={{0,1},{1,0},{2,3},{3,2},{4,5},{5,4},{6,7},{7,6},{8,9},{9,8},{10,11... | collective-permute-start | bytes 1769480 | tf_op jit(solution)/shard_map/ppermute | solution.py:63
  106.4 26.4 %collective-permute-start.17 = (bf16[4,2,48,768]{3,2,1,0:T(8,128)(2,1)S(1)}, bf16[4,2,48,768]{3,2,1,0:T(8,128)(2,1)}, u32[]{:S(2)}, u32[]{:S(2)}) collective-permute-start(bf16[4,2,48,768]{3,2,1,0:T(8,128)(2,1)S(1)} %collective-permute-done.15.refs_1_), channel_id=1, source_target_pairs={{0,1},{1,0},{2,3},{3,2},{4,5},{5,4},{6,7},{7,6},{8,9},{9,8},{10,11... | collective-permute-start | bytes 1769480 | tf_op jit(solution)/shard_map/ppermute | solution.py:64
  106.7 24.5 %collective-permute-start.21 = (bf16[4,1,48,768]{3,2,1,0:T(8,128)(2,1)S(1)}, bf16[4,1,48,768]{3,2,1,0:T(8,128)(2,1)S(1)}, u32[]{:S(2)}, u32[]{:S(2)}) collective-permute-start(bf16[4,1,48,768]{3,2,1,0:T(8,128)(2,1)S(1)} %pad_maximum_fusion.7.refs_2_), channel_id=1, source_target_pairs={{0,2},{1,3},{2,0},{3,1},{4,6},{5,7},{6,4},{7,5},{8,10},{9,11},{10,... | collective-permute-start | bytes 884744 | tf_op jit(solution)/shard_map/ppermute | solution.py:62
  107.3 39.5 %collective-permute-start.22 = (bf16[4,1,48,768]{3,2,1,0:T(8,128)(2,1)S(1)}, bf16[4,1,48,768]{3,2,1,0:T(8,128)(2,1)S(1)}, u32[]{:S(2)}, u32[]{:S(2)}) collective-permute-start(bf16[4,1,48,768]{3,2,1,0:T(8,128)(2,1)S(1)} %pad_maximum_fusion.7.refs_2_), channel_id=1, source_target_pairs={{0,1},{1,0},{2,3},{3,2},{4,5},{5,4},{6,7},{7,6},{8,9},{9,8},{10,11... | collective-permute-start | bytes 884744 | tf_op jit(solution)/shard_map/ppermute | solution.py:63
  131.2 28.4 %collective-permute-start.34 = (bf16[4,4,48,768]{3,2,1,0:T(8,128)(2,1)S(1)}, bf16[4,4,48,768]{3,2,1,0:T(8,128)(2,1)S(1)}, u32[]{:S(2)}, u32[]{:S(2)}) collective-permute-start(bf16[4,4,48,768]{3,2,1,0:T(8,128)(2,1)S(1)} %pad_maximum_fusion.1.refs_0_), channel_id=1, source_target_pairs={{0,1},{1,0},{2,3},{3,2},{4,5},{5,4},{6,7},{7,6},{8,9},{9,8},{10,11... | collective-permute-start | bytes 3538952 | tf_op jit(solution)/shard_map/ppermute | solution.py:63
  131.3 28.4 %collective-permute-start.27 = (bf16[4,4,48,768]{3,2,1,0:T(8,128)(2,1)S(1)}, bf16[4,4,48,768]{3,2,1,0:T(8,128)(2,1)S(1)}, u32[]{:S(2)}, u32[]{:S(2)}) collective-permute-start(bf16[4,4,48,768]{3,2,1,0:T(8,128)(2,1)S(1)} %pad_maximum_fusion.refs_0_), channel_id=1, source_target_pairs={{0,2},{1,3},{2,0},{3,1},{4,6},{5,7},{6,4},{7,5},{8,10},{9,11},{10,... | collective-permute-start | bytes 3538952 | tf_op jit(solution)/shard_map/ppermute | solution.py:62
  132.8 14.4 %collective-permute-start.23 = (bf16[4,1,48,768]{3,2,1,0:T(8,128)(2,1)S(1)}, bf16[4,1,48,768]{3,2,1,0:T(8,128)(2,1)S(1)}, u32[]{:S(2)}, u32[]{:S(2)}) collective-permute-start(bf16[4,1,48,768]{3,2,1,0:T(8,128)(2,1)S(1)} %collective-permute-done.21.refs_3_), channel_id=1, source_target_pairs={{0,1},{1,0},{2,3},{3,2},{4,5},{5,4},{6,7},{7,6},{8,9},{9,8},{10,11... | collective-permute-start | bytes 884744 | tf_op jit(solution)/shard_map/ppermute | solution.py:64
  133.0 26.7 %collective-permute-start.35 = (bf16[4,4,48,768]{3,2,1,0:T(8,128)(2,1)S(1)}, bf16[4,4,48,768]{3,2,1,0:T(8,128)(2,1)S(1)}, u32[]{:S(2)}, u32[]{:S(2)}) collective-permute-start(bf16[4,4,48,768]{3,2,1,0:T(8,128)(2,1)S(1)} %collective-permute-done.33.refs_1_), channel_id=1, source_target_pairs={{0,1},{1,0},{2,3},{3,2},{4,5},{5,4},{6,7},{7,6},{8,9},{9,8},{10,11... | collective-permute-start | bytes 3538952 | tf_op jit(solution)/shard_map/ppermute | solution.py:64
  146.8 43.4 %collective-permute-start.28 = (bf16[4,4,48,768]{3,2,1,0:T(8,128)(2,1)S(1)}, bf16[4,4,48,768]{3,2,1,0:T(8,128)(2,1)}, u32[]{:S(2)}, u32[]{:S(2)}) collective-permute-start(bf16[4,4,48,768]{3,2,1,0:T(8,128)(2,1)S(1)} %pad_maximum_fusion.refs_0_), channel_id=1, source_target_pairs={{0,1},{1,0},{2,3},{3,2},{4,5},{5,4},{6,7},{7,6},{8,9},{9,8},{10,11... | collective-permute-start | bytes 3538952 | tf_op jit(solution)/shard_map/ppermute | solution.py:63
  159.7 30.6 %collective-permute-start.29 = (bf16[4,4,48,768]{3,2,1,0:T(8,128)(2,1)S(1)}, bf16[4,4,48,768]{3,2,1,0:T(8,128)(2,1)}, u32[]{:S(2)}, u32[]{:S(2)}) collective-permute-start(bf16[4,4,48,768]{3,2,1,0:T(8,128)(2,1)S(1)} %collective-permute-done.27.refs_1_), channel_id=1, source_target_pairs={{0,1},{1,0},{2,3},{3,2},{4,5},{5,4},{6,7},{7,6},{8,9},{9,8},{10,11... | collective-permute-start | bytes 3538952 | tf_op jit(solution)/shard_map/ppermute | solution.py:64
  189.7 132.4 %collective-permute-start.54 = (bf16[2,4,4,48,768]{4,3,2,1,0:T(8,128)(2,1)}, bf16[2,4,4,48,768]{4,3,2,1,0:T(8,128)(2,1)S(1)}, u32[]{:S(2)}, u32[]{:S(2)}) collective-permute-start(bf16[2,4,4,48,768]{4,3,2,1,0:T(8,128)(2,1)} %get-tuple-element.99), channel_id=1, source_target_pairs={{0,1},{1,0},{2,3},{3,2},{4,5},{5,4},{6,7},{7,6},{8,9},{9,8},{10,11... | collective-permute-start | bytes 7077896 | tf_op jit(solution)/shard_map/ppermute | solution.py:77
  259.1 50.9 %collective-permute-start.48 = (bf16[2,4,3,48,768]{4,3,2,1,0:T(8,128)(2,1)}, bf16[2,4,3,48,768]{4,3,2,1,0:T(8,128)(2,1)}, u32[]{:S(2)}, u32[]{:S(2)}) collective-permute-start(bf16[2,4,3,48,768]{4,3,2,1,0:T(8,128)(2,1)} %get-tuple-element.97), channel_id=1, source_target_pairs={{0,1},{1,0},{2,3},{3,2},{4,5},{5,4},{6,7},{7,6},{8,9},{9,8},{10,11... | collective-permute-start | bytes 5308424 | tf_op jit(solution)/shard_map/ppermute | solution.py:77
  286.8 41.6 %collective-permute-start.60 = (bf16[2,4,4,48,768]{4,3,2,1,0:T(8,128)(2,1)}, bf16[2,4,4,48,768]{4,3,2,1,0:T(8,128)(2,1)S(1)}, u32[]{:S(2)}, u32[]{:S(2)}) collective-permute-start(bf16[2,4,4,48,768]{4,3,2,1,0:T(8,128)(2,1)} %get-tuple-element.101), channel_id=1, source_target_pairs={{0,1},{1,0},{2,3},{3,2},{4,5},{5,4},{6,7},{7,6},{8,9},{9,8},{10,11... | collective-permute-start | bytes 7077896 | tf_op jit(solution)/shard_map/ppermute | solution.py:77
  287.6 3.7 collective-permute-start.37
  289.1 18.0 %collective-permute-start.42 = (bf16[2,4,1,48,768]{4,3,2,1,0:T(8,128)(2,1)}, bf16[2,4,1,48,768]{4,3,2,1,0:T(8,128)(2,1)S(1)}, u32[]{:S(2)}, u32[]{:S(2)}) collective-permute-start(bf16[2,4,1,48,768]{4,3,2,1,0:T(8,128)(2,1)} %get-tuple-element.95), channel_id=1, source_target_pairs={{0,1},{1,0},{2,3},{3,2},{4,5},{5,4},{6,7},{7,6},{8,9},{9,8},{10,11... | collective-permute-start | bytes 1769480 | tf_op jit(solution)/shard_map/ppermute | solution.py:77
  291.4 3.6 collective-permute-start.38
  295.0 4.8 %collective-permute-start.39 = (f32[8,128]{1,0:T(8,128)S(1)}, f32[8,128]{1,0:T(8,128)S(1)}, u32[]{:S(2)}, u32[]{:S(2)}) collective-permute-start(f32[8,128]{1,0:T(8,128)S(1)} %get-tuple-element.120), channel_id=1, source_target_pairs={{0,8},{1,9},{2,10},{3,11},{4,12},{5,13},{6,14},{7,15},{8,0},{9,1},... | collective-permute-start | bytes 12296 | tf_op jit(solution)/shard_map/ppermute | solution.py:83
  299.8 3.7 collective-permute-start.40
  303.5 3.6 collective-permute-start.41
  307.2 10.0 %collective-permute-start.43 = (bf16[4,1,48,768]{3,2,1,0:T(8,128)(2,1)S(1)}, bf16[4,1,48,768]{3,2,1,0:T(8,128)(2,1)S(1)}, u32[]{:S(2)}, u32[]{:S(2)}) collective-permute-start(bf16[4,1,48,768]{3,2,1,0:T(8,128)(2,1)S(1)} %fusion.15), channel_id=1, source_target_pairs={{0,2},{1,3},{2,0},{3,1},{4,6},{5,7},{6,4},{7,5},{8,10},{9,11},{10,... | collective-permute-start | bytes 884744 | tf_op jit(solution)/shard_map/ppermute | solution.py:79
  311.6 24.6 %collective-permute-start.49 = (bf16[4,3,48,768]{3,2,1,0:T(8,128)(2,1)S(1)}, bf16[4,3,48,768]{3,2,1,0:T(8,128)(2,1)S(1)}, u32[]{:S(2)}, u32[]{:S(2)}) collective-permute-start(bf16[4,3,48,768]{3,2,1,0:T(8,128)(2,1)S(1)} %fusion.2), channel_id=1, source_target_pairs={{0,2},{1,3},{2,0},{3,1},{4,6},{5,7},{6,4},{7,5},{8,10},{9,11},{10,... | collective-permute-start | bytes 2654216 | tf_op jit(solution)/shard_map/ppermute | solution.py:79
  317.3 7.3 %collective-permute-start.44 = (bf16[1,48,768]{2,1,0:T(8,128)(2,1)S(1)}, bf16[1,48,768]{2,1,0:T(8,128)(2,1)S(1)}, u32[]{:S(2)}, u32[]{:S(2)}) collective-permute-start(bf16[1,48,768]{2,1,0:T(8,128)(2,1)S(1)} %get-tuple-element.111), channel_id=1, source_target_pairs={{0,4},{1,5},{2,6},{3,7},{4,8},{5,9},{6,10},{7,11},{8,12},{9,13},{1... | collective-permute-start | bytes 221192 | tf_op jit(solution)/shard_map/ppermute | solution.py:83
  318.8 7.4 %collective-permute-start.45 = (bf16[1,48,768]{2,1,0:T(8,128)(2,1)S(1)}, bf16[1,48,768]{2,1,0:T(8,128)(2,1)S(1)}, u32[]{:S(2)}, u32[]{:S(2)}) collective-permute-start(bf16[1,48,768]{2,1,0:T(8,128)(2,1)S(1)} %get-tuple-element.113), channel_id=1, source_target_pairs={{0,8},{1,9},{2,10},{3,11},{4,12},{5,13},{6,14},{7,15},{8,0},{9,1},... | collective-permute-start | bytes 221192 | tf_op jit(solution)/shard_map/ppermute | solution.py:83
  322.1 4.6 %collective-permute-start.46 = (bf16[1,48,768]{2,1,0:T(8,128)(2,1)S(1)}, bf16[1,48,768]{2,1,0:T(8,128)(2,1)S(1)}, u32[]{:S(2)}, u32[]{:S(2)}) collective-permute-start(bf16[1,48,768]{2,1,0:T(8,128)(2,1)S(1)} %get-tuple-element.112), channel_id=1, source_target_pairs={{0,12},{1,13},{2,14},{3,15},{4,0},{5,1},{6,2},{7,3},{8,4},{9,5},{1... | collective-permute-start | bytes 221192 | tf_op jit(solution)/shard_map/ppermute | solution.py:83
  324.6 36.9 %collective-permute-start.55 = (bf16[4,4,48,768]{3,2,1,0:T(8,128)(2,1)S(1)}, bf16[4,4,48,768]{3,2,1,0:T(8,128)(2,1)S(1)}, u32[]{:S(2)}, u32[]{:S(2)}) collective-permute-start(bf16[4,4,48,768]{3,2,1,0:T(8,128)(2,1)S(1)} %fusion), channel_id=1, source_target_pairs={{0,2},{1,3},{2,0},{3,1},{4,6},{5,7},{6,4},{7,5},{8,10},{9,11},{10,... | collective-permute-start | bytes 3538952 | tf_op jit(solution)/shard_map/ppermute | solution.py:79
  326.8 15.6 %collective-permute-start.47 = (bf16[1,48,768]{2,1,0:T(8,128)(2,1)S(1)}, bf16[1,48,768]{2,1,0:T(8,128)(2,1)S(1)}, u32[]{:S(2)}, u32[]{:S(2)}) collective-permute-start(bf16[1,48,768]{2,1,0:T(8,128)(2,1)S(1)} %add_convert_fusion.7), channel_id=1, source_target_pairs={{0,16},{16,0},{1,17},{17,1},{2,18},{18,2},{3,19},{19,3},{4,20},{20... | collective-permute-start | bytes 221192 | tf_op jit(solution)/shard_map/ppermute | solution.py:85
  328.7 53.1 %collective-permute-start.61 = (bf16[4,4,48,768]{3,2,1,0:T(8,128)(2,1)S(1)}, bf16[4,4,48,768]{3,2,1,0:T(8,128)(2,1)S(1)}, u32[]{:S(2)}, u32[]{:S(2)}) collective-permute-start(bf16[4,4,48,768]{3,2,1,0:T(8,128)(2,1)S(1)} %fusion.1), channel_id=1, source_target_pairs={{0,2},{1,3},{2,0},{3,1},{4,6},{5,7},{6,4},{7,5},{8,10},{9,11},{10,... | collective-permute-start | bytes 3538952 | tf_op jit(solution)/shard_map/ppermute | solution.py:79
  337.6 6.7 %collective-permute-start.50 = (bf16[3,48,768]{2,1,0:T(8,128)(2,1)S(1)}, bf16[3,48,768]{2,1,0:T(8,128)(2,1)S(1)}, u32[]{:S(2)}, u32[]{:S(2)}) collective-permute-start(bf16[3,48,768]{2,1,0:T(8,128)(2,1)S(1)} %get-tuple-element.108), channel_id=1, source_target_pairs={{0,4},{1,5},{2,6},{3,7},{4,8},{5,9},{6,10},{7,11},{8,12},{9,13},{1... | collective-permute-start | bytes 663560 | tf_op jit(solution)/shard_map/ppermute | solution.py:83
  339.0 11.6 %collective-permute-start.51 = (bf16[3,48,768]{2,1,0:T(8,128)(2,1)S(1)}, bf16[3,48,768]{2,1,0:T(8,128)(2,1)S(1)}, u32[]{:S(2)}, u32[]{:S(2)}) collective-permute-start(bf16[3,48,768]{2,1,0:T(8,128)(2,1)S(1)} %get-tuple-element.110), channel_id=1, source_target_pairs={{0,8},{1,9},{2,10},{3,11},{4,12},{5,13},{6,14},{7,15},{8,0},{9,1},... | collective-permute-start | bytes 663560 | tf_op jit(solution)/shard_map/ppermute | solution.py:83
  342.4 11.0 %collective-permute-start.52 = (bf16[3,48,768]{2,1,0:T(8,128)(2,1)S(1)}, bf16[3,48,768]{2,1,0:T(8,128)(2,1)S(1)}, u32[]{:S(2)}, u32[]{:S(2)}) collective-permute-start(bf16[3,48,768]{2,1,0:T(8,128)(2,1)S(1)} %get-tuple-element.109), channel_id=1, source_target_pairs={{0,12},{1,13},{2,14},{3,15},{4,0},{5,1},{6,2},{7,3},{8,4},{9,5},{1... | collective-permute-start | bytes 663560 | tf_op jit(solution)/shard_map/ppermute | solution.py:83
  354.5 8.8 %collective-permute-start.53 = (bf16[3,48,768]{2,1,0:T(8,128)(2,1)S(1)}, bf16[3,48,768]{2,1,0:T(8,128)(2,1)S(1)}, u32[]{:S(2)}, u32[]{:S(2)}) collective-permute-start(bf16[3,48,768]{2,1,0:T(8,128)(2,1)S(1)} %add_convert_fusion.6), channel_id=1, source_target_pairs={{0,16},{16,0},{1,17},{17,1},{2,18},{18,2},{3,19},{19,3},{4,20},{20... | collective-permute-start | bytes 663560 | tf_op jit(solution)/shard_map/ppermute | solution.py:85
  361.8 25.0 %collective-permute-start.56 = (bf16[4,48,768]{2,1,0:T(8,128)(2,1)S(1)}, bf16[4,48,768]{2,1,0:T(8,128)(2,1)S(1)}, u32[]{:S(2)}, u32[]{:S(2)}) collective-permute-start(bf16[4,48,768]{2,1,0:T(8,128)(2,1)S(1)} %get-tuple-element.102), channel_id=1, source_target_pairs={{0,4},{1,5},{2,6},{3,7},{4,8},{5,9},{6,10},{7,11},{8,12},{9,13},{1... | collective-permute-start | bytes 884744 | tf_op jit(solution)/shard_map/ppermute | solution.py:83
  363.3 25.7 %collective-permute-start.57 = (bf16[4,48,768]{2,1,0:T(8,128)(2,1)S(1)}, bf16[4,48,768]{2,1,0:T(8,128)(2,1)S(1)}, u32[]{:S(2)}, u32[]{:S(2)}) collective-permute-start(bf16[4,48,768]{2,1,0:T(8,128)(2,1)S(1)} %get-tuple-element.104), channel_id=1, source_target_pairs={{0,8},{1,9},{2,10},{3,11},{4,12},{5,13},{6,14},{7,15},{8,0},{9,1},... | collective-permute-start | bytes 884744 | tf_op jit(solution)/shard_map/ppermute | solution.py:83
  366.7 22.3 %collective-permute-start.58 = (bf16[4,48,768]{2,1,0:T(8,128)(2,1)S(1)}, bf16[4,48,768]{2,1,0:T(8,128)(2,1)S(1)}, u32[]{:S(2)}, u32[]{:S(2)}) collective-permute-start(bf16[4,48,768]{2,1,0:T(8,128)(2,1)S(1)} %get-tuple-element.103), channel_id=1, source_target_pairs={{0,12},{1,13},{2,14},{3,15},{4,0},{5,1},{6,2},{7,3},{8,4},{9,5},{1... | collective-permute-start | bytes 884744 | tf_op jit(solution)/shard_map/ppermute | solution.py:83
  382.2 18.8 %collective-permute-start.62 = (bf16[4,48,768]{2,1,0:T(8,128)(2,1)S(1)}, bf16[4,48,768]{2,1,0:T(8,128)(2,1)S(1)}, u32[]{:S(2)}, u32[]{:S(2)}) collective-permute-start(bf16[4,48,768]{2,1,0:T(8,128)(2,1)S(1)} %get-tuple-element.105), channel_id=1, source_target_pairs={{0,4},{1,5},{2,6},{3,7},{4,8},{5,9},{6,10},{7,11},{8,12},{9,13},{1... | collective-permute-start | bytes 884744 | tf_op jit(solution)/shard_map/ppermute | solution.py:83
  383.5 20.6 %collective-permute-start.63 = (bf16[4,48,768]{2,1,0:T(8,128)(2,1)S(1)}, bf16[4,48,768]{2,1,0:T(8,128)(2,1)S(1)}, u32[]{:S(2)}, u32[]{:S(2)}) collective-permute-start(bf16[4,48,768]{2,1,0:T(8,128)(2,1)S(1)} %get-tuple-element.107), channel_id=1, source_target_pairs={{0,8},{1,9},{2,10},{3,11},{4,12},{5,13},{6,14},{7,15},{8,0},{9,1},... | collective-permute-start | bytes 884744 | tf_op jit(solution)/shard_map/ppermute | solution.py:83
  386.9 20.7 %collective-permute-start.64 = (bf16[4,48,768]{2,1,0:T(8,128)(2,1)S(1)}, bf16[4,48,768]{2,1,0:T(8,128)(2,1)S(1)}, u32[]{:S(2)}, u32[]{:S(2)}) collective-permute-start(bf16[4,48,768]{2,1,0:T(8,128)(2,1)S(1)} %get-tuple-element.106), channel_id=1, source_target_pairs={{0,12},{1,13},{2,14},{3,15},{4,0},{5,1},{6,2},{7,3},{8,4},{9,5},{1... | collective-permute-start | bytes 884744 | tf_op jit(solution)/shard_map/ppermute | solution.py:83
  389.2 21.8 %collective-permute-start.59 = (bf16[4,48,768]{2,1,0:T(8,128)(2,1)S(1)}, bf16[4,48,768]{2,1,0:T(8,128)(2,1)S(1)}, u32[]{:S(2)}, u32[]{:S(2)}) collective-permute-start(bf16[4,48,768]{2,1,0:T(8,128)(2,1)S(1)} %add_convert_fusion.4), channel_id=1, source_target_pairs={{0,16},{16,0},{1,17},{17,1},{2,18},{18,2},{3,19},{19,3},{4,20},{20... | collective-permute-start | bytes 884744 | tf_op jit(solution)/shard_map/ppermute | solution.py:85
  407.8 8.5 %collective-permute-start.65 = (bf16[4,48,768]{2,1,0:T(8,128)(2,1)S(1)}, bf16[4,48,768]{2,1,0:T(8,128)(2,1)S(1)}, u32[]{:S(2)}, u32[]{:S(2)}) collective-permute-start(bf16[4,48,768]{2,1,0:T(8,128)(2,1)S(1)} %add_convert_fusion.3), channel_id=1, source_target_pairs={{0,16},{16,0},{1,17},{17,1},{2,18},{18,2},{3,19},{19,3},{4,20},{20... | collective-permute-start | bytes 884744 | tf_op jit(solution)/shard_map/ppermute | solution.py:85
  (30 other events, 434.8 us)
